TPU v7x, 32 devices: a whole 2x2x4 slice. The times are simulated.
32 devices in a mesh: groups: 2 (over x), mesh: 16 (over z, y, core).
Axes of the slice: x: 2, y: 2, z: 4, core: 2. Of those that a mesh axis runs over, the one named last changes fastest.
Arguments:
- water_depth: float32 [768, 10, 640], P(('groups', 'mesh')), parts along dimension 0, may hold values from 1 to 3
- momentum: float32 [768, 2, 10, 640], P(('groups', 'mesh')), parts along dimension 0, may hold values from -3 to 3
- metric: float32 [768, 4, 64], P(('groups', 'mesh')), parts along dimension 0, may hold values from -2 to 2
- face_scale: float32 [768, 192], P(('groups', 'mesh')), parts along dimension 0, may hold values from 0.5 to 2
- face_angle: float32 [768, 192], P(('groups', 'mesh')), parts along dimension 0, may hold values from -3.140625 to 3.140625
- face_map: int32 [768, 192], P(('groups', 'mesh')), parts along dimension 0, may hold values from 0 to 4735, as said below
- rim_faces: int32 [32, 128], P(('groups', 'mesh')), parts along dimension 0, may hold values from 0 to 4607, as said below
- wet_blocks: int32 [768], P(('groups', 'mesh')), parts along dimension 0, may hold values from 0 to 1, as said below
- breach: int32 [768, 10], P(('groups', 'mesh')), parts along dimension 0, may hold values from 0 to 3
- block_plan: int32 [768], P('groups'), parts along dimension 0, may hold values from 0 to 383, as said below
Outputs:
- depth_out: float32 [768, 10, 640], P(('groups', 'mesh')), parts along dimension 0
- momentum_out: float32 [768, 2, 10, 640], P(('groups', 'mesh')), parts along dimension 0
There are 2 independent parts, one for each index of `groups`. A program takes and returns all parts, laid end to end along the dimension named above; each array names one. Nothing has to cross between parts.
Inputs may be any that keep to these rules, and one draw needn't show every extreme that they name: `face_map`: The rim entries pair in order: entry i of index d's second half of rim_faces with entry i of index d + 1's first half. No face of the first index names a previous index, none of the last a next one. `rim_faces`: each row holds 128 distinct local face numbers. `wet_blocks`: every block of mesh index 0 is 1; the chance of a 1 falls along the mesh axis. `block_plan`: A permutation of the block slots. Each mesh index hands exactly 8 of its blocks to other indices, each to a different index, and receives exactly 8, each from a different index, into the slots it vacates; the other blocks stay.
All inputs are finite; a program needn't handle non-finite values.
Results may differ from a plain program's by a relative error of at most 0.000059.
Values sent between devices are 32-bit elements; how exact they have to be, the bound alone decides.
A program may use at most 192 MiB of HBM per device.

v0:
```python
import math

import jax
import jax.numpy as jnp
import numpy as np
import ml_dtypes
from jax import lax
from jax.experimental import pallas as pl
from jax.experimental.pallas import tpu as pltpu
from jax.sharding import PartitionSpec as P

time_step = 0.01
gravity = 1.0
breach_rate = 5.0


SMEM = pl.BlockSpec(memory_space=pltpu.SMEM)
VMEM = pl.BlockSpec(memory_space=pltpu.VMEM)
ANY = pl.BlockSpec(memory_space=pl.ANY)
faces, face_points = 3, 4


def gauss_solve(matrix, right):
    dimension = matrix.shape[0]
    augmented = np.concatenate([np.array(matrix) * 1.0, np.array(right) * 1.0], axis=1)
    for pivot_col in range(dimension):
        largest = pivot_col + int(np.argmax(np.abs(augmented[pivot_col:, pivot_col])))
        swapped = augmented[[largest, pivot_col]]
        augmented[[pivot_col, largest]] = swapped
        augmented[pivot_col] = augmented[pivot_col] / augmented[pivot_col, pivot_col]
        for row_id in range(dimension):
            if row_id != pivot_col:
                augmented[row_id] = (
                    augmented[row_id] - augmented[row_id, pivot_col] * augmented[pivot_col]
                )
    return augmented[:, dimension:]


def node_tables():
    points = np.array(
        [(across / 3.0, upward / 3.0) for upward in range(4) for across in range(4 - upward)]
    )
    powers = [(power_r, power_s) for power_r in range(4) for power_s in range(4 - power_r)]
    vander = np.zeros((10, 10))
    grad_r = np.zeros((10, 10))
    grad_s = np.zeros((10, 10))
    mono_mass = np.zeros((10, 10))
    for column, (power_r, power_s) in enumerate(powers):
        vander[:, column] = points[:, 0] ** power_r * points[:, 1] ** power_s
        if power_r > 0:
            grad_r[:, column] = power_r * points[:, 0] ** (power_r - 1) * points[:, 1] ** power_s
        if power_s > 0:
            grad_s[:, column] = power_s * points[:, 0] ** power_r * points[:, 1] ** (power_s - 1)
        for second_column, (other_r, other_s) in enumerate(powers):
            mono_mass[column, second_column] = (
                math.factorial(power_r + other_r)
                * math.factorial(power_s + other_s)
                / math.factorial(power_r + other_r + power_s + other_s + 2)
            )
    inverse = gauss_solve(vander, np.eye(10))
    mass_matrix = inverse.T @ mono_mass @ inverse
    line_points = np.arange(4) / 3.0
    line_vander = line_points[:, None] ** np.arange(4)[None, :]
    hilbert = 1.0 / (np.arange(4)[:, None] + np.arange(4)[None, :] + 1.0)
    line_inverse = gauss_solve(line_vander, np.eye(4))
    edge_mass = line_inverse.T @ hilbert @ line_inverse
    face_nodes = np.array([[0, 1, 2, 3], [3, 6, 8, 9], [9, 7, 4, 0]])
    edge_embed = np.zeros((10, 12))
    for face_id in range(3):
        for node_id in range(4):
            edge_embed[face_nodes[face_id, node_id], 4 * face_id : 4 * face_id + 4] += edge_mass[
                node_id
            ]
    lifting = gauss_solve(mass_matrix, edge_embed).reshape(10, 3, 4)
    return (
        np.asarray(grad_r @ inverse, np.float32),
        np.asarray(grad_s @ inverse, np.float32),
        np.asarray(lifting, np.float32),
        face_nodes,
    )


def round_up(count, step):
    return -(-count // step) * step


def combined_matrix(members, rows, node_count):
    deriv_r, deriv_s, lifting, _ = node_tables()
    full = members // 8 * 8
    rest = members - full
    face_rows = face_points * members
    columns = 2 * rows + round_up(faces * face_rows, 16)

    def place(point, member, points):
        if member < full:
            return point * full + member
        return points * full + point * rest + member - full

    table = np.zeros((rows, columns), np.float32)
    for member in range(members):
        for node in range(node_count):
            row = place(node, member, node_count)
            for other in range(node_count):
                column = place(other, member, node_count)
                table[row, column] = -deriv_r[node, other]
                table[row, rows + column] = -deriv_s[node, other]
            for face in range(faces):
                for point in range(face_points):
                    column = 2 * rows + face * face_rows + place(point, member, face_points)
                    table[row, column] = lifting[node, face, point]
    high = table.astype(ml_dtypes.bfloat16)
    low = (table - high.astype(np.float32)).astype(ml_dtypes.bfloat16)
    return high, low


def lanes_low(shape, elements):
    return lax.broadcasted_iota(jnp.int32, shape, len(shape) - 1) < elements


def stack_face(fields_ref, pair, comp, nodes, members, node_count, out_ref, start):
    full = members // 8 * 8
    rest = members - full
    for point, node in enumerate(nodes):
        out_ref[start + point * full : start + (point + 1) * full, :] = fields_ref[
            pair, comp, node * full : (node + 1) * full, :
        ]
    base = node_count * full
    tail = start + len(nodes) * full
    for point, node in enumerate(nodes):
        out_ref[tail + point * rest : tail + (point + 1) * rest, :] = fields_ref[
            pair, comp, base + node * rest : base + (node + 1) * rest, :
        ]


def layout_kernel(
    face_nodes, node_count, depth_ref, flow_ref, rim_ref, fields_ref, table_ref, edge_ref, stack_ref
):
    blocks, members, node_cells = depth_ref.shape
    elements = node_cells // node_count
    lanes = 2 * elements
    full = members // 8 * 8
    rest = members - full
    used = node_count * members
    rows = fields_ref.shape[2]
    face_rows = face_points * members
    stack_ref[...] = jnp.zeros_like(stack_ref)

    def one_pair(pair, carry):
        for comp in range(3):
            fields_ref[pair, comp, used:rows, :] = jnp.ones((rows - used, lanes), jnp.float32)
            for half in range(node_count // 2):
                for first, size in ((0, full), (full, rest)):
                    cells = (pl.ds(first, size), pl.ds(half * lanes, lanes))
                    if comp == 0:
                        one = depth_ref[(2 * pair, *cells)]
                        two = depth_ref[(2 * pair + 1, *cells)]
                    else:
                        one = flow_ref[(2 * pair, comp - 1, *cells)]
                        two = flow_ref[(2 * pair + 1, comp - 1, *cells)]
                    low = lanes_low(one.shape, elements)
                    base = node_count * first + 2 * half * size
                    fields_ref[pair, comp, base : base + size, :] = jnp.where(
                        low, one, pltpu.roll(two, elements, 1)
                    )
                    fields_ref[pair, comp, base + size : base + 2 * size, :] = jnp.where(
                        low, pltpu.roll(one, elements, 1), two
                    )
        for face in range(faces):
            nodes = [int(node) for node in face_nodes[face][::-1]]
            for comp in range(3):
                stack_face(
                    fields_ref, pair, comp, nodes, members, node_count,
                    stack_ref.at[face], comp * face_rows,
                )
            turned = stack_ref[face].T
            start = pl.multiple_of((2 * pair * faces + face) * elements, 8)
            table_ref[pl.ds(start, elements), :] = turned[:elements]
            start = pl.multiple_of(((2 * pair + 1) * faces + face) * elements, 8)
            table_ref[pl.ds(start, elements), :] = turned[elements:]
        return carry

    lax.fori_loop(0, blocks // 2, one_pair, 0)
    rim_count = rim_ref.shape[1]

    def one_group(group, carry):
        for step in range(16):
            face = group * 16 + step
            edge_ref[pl.ds(face, 1), :] = table_ref[pl.ds(rim_ref[0, face], 1), :]
        return carry

    lax.fori_loop(0, rim_count // 16, one_group, 0)


def advance_kernel(
    face_nodes, node_count, members, low_start,
    own_ref, map_ref, wet_ref, breach_ref, plan_ref,
    fields_ref, table_ref, before_ref, after_ref,
    metric_ref, scale_ref, angle_ref, links_ref, high_ref, low_ref,
    depth_out, flow_out, send_ref,
    pool_ref, picked_ref, inner_ref, cos_ref, sin_ref, wall_ref, right_ref, chosen_ref, sems,
):
    blocks = depth_out.shape[0]
    elements = metric_ref.shape[2]
    lanes = 2 * elements
    rows = fields_ref.shape[2]
    full = members // 8 * 8
    rest = members - full
    face_rows = face_points * members
    block_faces = faces * elements
    local_faces = blocks * block_faces
    rim = before_ref.shape[0]
    copies = [
        pltpu.make_async_copy(table_ref, pool_ref.at[pl.ds(0, local_faces)], sems.at[0]),
        pltpu.make_async_copy(before_ref, pool_ref.at[pl.ds(local_faces, rim)], sems.at[1]),
        pltpu.make_async_copy(after_ref, pool_ref.at[pl.ds(local_faces + rim, rim)], sems.at[2]),
    ]
    for copy in copies:
        copy.start()

    angles = angle_ref[...]
    cos_ref[...] = jnp.cos(angles)
    sin_ref[...] = jnp.sin(angles)
    own_number = (
        lax.broadcasted_iota(jnp.int32, angles.shape, 0) * block_faces
        + lax.broadcasted_iota(jnp.int32, angles.shape, 1)
    )
    wall_ref[...] = jnp.where(links_ref[...] == own_number, 1.0, 0.0)
    right_ref[...] = jnp.zeros_like(right_ref)

    own = own_ref[0]

    def clear(index, carry):
        chosen_ref[index] = 0
        return carry

    lax.fori_loop(0, chosen_ref.shape[0], clear, 0)

    def choose(index, carry):
        target = plan_ref[own * blocks + index] // blocks

        @pl.when(target != own)
        def _():
            chosen_ref[target] = index

        return carry

    lax.fori_loop(0, blocks, choose, 0)
    for copy in copies:
        copy.wait()

    def one_pair(pair, carry):
        for side in range(2):
            for face in range(block_faces):
                picked_ref[side * block_faces + face : side * block_faces + face + 1, :] = pool_ref[
                    pl.ds(map_ref[2 * pair + side, face], 1), :
                ]

        def face_row(ref, face):
            first = ref[pl.ds(2 * pair, 1), :]
            second = ref[pl.ds(2 * pair + 1, 1), :]
            cells = slice(face * elements, (face + 1) * elements)
            return jnp.concatenate([first[:, cells], second[:, cells]], axis=1)

        for face in range(faces):
            nodes = [int(node) for node in face_nodes[face]]
            for comp in range(3):
                stack_face(
                    fields_ref, pair, comp, nodes, members, node_count,
                    inner_ref.at[face], comp * face_rows,
                )
            height = inner_ref[face, 0:face_rows]
            flow_x = inner_ref[face, face_rows : 2 * face_rows]
            flow_y = inner_ref[face, 2 * face_rows : 3 * face_rows]
            outside = jnp.concatenate(
                [
                    picked_ref[face * elements : (face + 1) * elements],
                    picked_ref[block_faces + face * elements : block_faces + (face + 1) * elements],
                ],
                axis=0,
            ).T
            normal_x = face_row(cos_ref, face)
            normal_y = face_row(sin_ref, face)
            wall = face_row(wall_ref, face) > 0.5
            half_scale = 0.5 * face_row(scale_ref, face)
            flow = flow_x * normal_x + flow_y * normal_y
            out_height = jnp.where(wall, height, outside[0:face_rows])
            out_x = jnp.where(
                wall, flow_x - 2.0 * flow * normal_x, outside[face_rows : 2 * face_rows]
            )
            out_y = jnp.where(
                wall, flow_y - 2.0 * flow * normal_y, outside[2 * face_rows : 3 * face_rows]
            )
            out_flow = out_x * normal_x + out_y * normal_y
            speed = flow / height
            out_speed = out_flow / out_height
            wave = jnp.maximum(
                jnp.abs(speed) + jnp.sqrt(gravity * height),
                jnp.abs(out_speed) + jnp.sqrt(gravity * out_height),
            )
            pressure = 0.5 * gravity * (height * height - out_height * out_height)
            jumps = (
                flow - out_flow + wave * (out_height - height),
                flow_x * speed - out_x * out_speed + pressure * normal_x + wave * (out_x - flow_x),
                flow_y * speed - out_y * out_speed + pressure * normal_y + wave * (out_y - flow_y),
            )
            start = 2 * rows + face * face_rows
            for comp in range(3):
                right_ref[start : start + face_rows, comp * lanes : (comp + 1) * lanes] = (
                    half_scale * jumps[comp]
                )

        factors = jnp.concatenate([metric_ref[2 * pair], metric_ref[2 * pair + 1]], axis=1)
        height = fields_ref[pair, 0]
        flow_x = fields_ref[pair, 1]
        flow_y = fields_ref[pair, 2]
        inverse = 1.0 / height
        pressure = 0.5 * gravity * height * height
        speed_x = flow_x * inverse
        speed_y = flow_y * inverse
        cross = flow_x * speed_y
        flux_f = (flow_x, flow_x * speed_x + pressure, cross)
        flux_g = (flow_y, cross, flow_y * speed_y + pressure)
        for comp in range(3):
            span = slice(comp * lanes, (comp + 1) * lanes)
            right_ref[0:rows, span] = factors[0:1] * flux_f[comp] + factors[2:3] * flux_g[comp]
            right_ref[rows : 2 * rows, span] = (
                factors[1:2] * flux_f[comp] + factors[3:4] * flux_g[comp]
            )
        right = right_ref[...]
        right_high = right.astype(jnp.bfloat16)
        right_low = (right - right_high.astype(jnp.float32)).astype(jnp.bfloat16)
        high = high_ref[...]
        tendency = (
            jnp.dot(high, right_high, preferred_element_type=jnp.float32)
            + jnp.dot(high, right_low, preferred_element_type=jnp.float32)
            + jnp.dot(
                low_ref[...], right_high[low_start:], preferred_element_type=jnp.float32
            )
        )
        row_low = lanes_low((1, lanes), elements)
        step = time_step * jnp.where(
            row_low, wet_ref[2 * pair].astype(jnp.float32), wet_ref[2 * pair + 1].astype(jnp.float32)
        )

        def inflow(member):
            return breach_rate * jnp.where(
                row_low,
                breach_ref[2 * pair, member].astype(jnp.float32),
                breach_ref[2 * pair + 1, member].astype(jnp.float32),
            )

        def inflow_rows(first, size):
            row_ids = lax.broadcasted_iota(jnp.int32, (size, lanes), 0)
            total = jnp.zeros((size, lanes), jnp.float32)
            for member in range(size):
                total = jnp.where(row_ids == member, inflow(first + member), total)
            return total

        for first, size in ((0, full), (full, rest)):
            source = inflow_rows(first, size)
            low = lanes_low((size, lanes), elements)
            for comp in range(3):
                span = slice(comp * lanes, (comp + 1) * lanes)
                for half in range(node_count // 2):
                    both = []
                    for side in range(2):
                        base = node_count * first + (2 * half + side) * size
                        change = tendency[base : base + size, span]
                        if comp == 0:
                            change = change + source
                        both.append(fields_ref[pair, comp, base : base + size, :] + step * change)
                    one = jnp.where(low, both[0], pltpu.roll(both[1], elements, 1))
                    two = jnp.where(low, pltpu.roll(both[0], elements, 1), both[1])
                    cells = (pl.ds(first, size), pl.ds(half * lanes, lanes))
                    if comp == 0:
                        depth_out[(2 * pair, *cells)] = one
                        depth_out[(2 * pair + 1, *cells)] = two
                    else:
                        flow_out[(2 * pair, comp - 1, *cells)] = one
                        flow_out[(2 * pair + 1, comp - 1, *cells)] = two
        return carry

    lax.fori_loop(0, blocks // 2, one_pair, 0)

    def one_send(device, carry):
        block = chosen_ref[device]
        for comp in range(3):
            for first, size in ((0, full), (full, rest)):
                base = 3 * first + comp * size
                if comp == 0:
                    value = depth_out[block, first : first + size, :]
                else:
                    value = flow_out[block, comp - 1, first : first + size, :]
                send_ref[device, base : base + size, :] = value
        return carry

    lax.fori_loop(0, send_ref.shape[0], one_send, 0)


def merge_kernel(source_ref, own_ref, got_ref, depth_ref, flow_ref, depth_out, flow_out):
    blocks, members, _ = depth_ref.shape
    full = members // 8 * 8
    rest = members - full

    def one_slot(slot, carry):
        source = source_ref[slot]

        @pl.when(source == own_ref[0])
        def _():
            depth_out[slot] = depth_ref[slot]
            flow_out[slot] = flow_ref[slot]

        @pl.when(source != own_ref[0])
        def _():
            for comp in range(3):
                for first, size in ((0, full), (full, rest)):
                    base = 3 * first + comp * size
                    value = got_ref[source, base : base + size, :]
                    if comp == 0:
                        depth_out[slot, first : first + size, :] = value
                    else:
                        flow_out[slot, comp - 1, first : first + size, :] = value

        return carry

    lax.fori_loop(0, blocks, one_slot, 0)


def body(
    water_depth,
    momentum,
    metric,
    face_scale,
    face_angle,
    face_map,
    rim_faces,
    wet_blocks,
    breach,
    block_plan,
):
    face_nodes = node_tables()[3]
    node_count = int(face_nodes.max()) + 1
    blocks, members, node_cells = water_depth.shape
    elements = node_cells // node_count
    lanes = 2 * elements
    rows = round_up(node_count * members, 16)
    block_faces = faces * elements
    local_faces = blocks * block_faces
    rim_count = rim_faces.shape[1]
    rim = rim_count // 2
    own_index = lax.axis_index("mesh")
    devices = lax.axis_size("mesh")
    params = pltpu.CompilerParams(vmem_limit_bytes=48 * 2**20)
    f32 = jnp.float32

    fields, table, edge = pl.pallas_call(
        lambda *refs: layout_kernel(face_nodes, node_count, *refs),
        out_shape=(
            jax.ShapeDtypeStruct((blocks // 2, 3, rows, lanes), f32),
            jax.ShapeDtypeStruct((local_faces, lanes), f32),
            jax.ShapeDtypeStruct((rim_count, lanes), f32),
        ),
        in_specs=[VMEM, VMEM, SMEM],
        out_specs=(VMEM, VMEM, VMEM),
        scratch_shapes=[pltpu.VMEM((faces, lanes, lanes), f32)],
        compiler_params=params,
    )(water_depth, momentum, rim_faces)

    ends = devices - 1
    from_before = lax.ppermute(edge[rim:], "mesh", [(i, i + 1) for i in range(ends)])
    from_after = lax.ppermute(edge[:rim], "mesh", [(i + 1, i) for i in range(ends)])

    high, low = combined_matrix(members, rows, node_count)
    low_start = 2 * rows if not np.any(low[:, : 2 * rows].astype(np.float32)) else 0
    own = jnp.reshape(own_index.astype(jnp.int32), (1,))
    send_rows = round_up(3 * members, 8)
    depth, flow, send = pl.pallas_call(
        lambda *refs: advance_kernel(face_nodes, node_count, members, low_start, *refs),
        out_shape=(
            jax.ShapeDtypeStruct(water_depth.shape, f32),
            jax.ShapeDtypeStruct(momentum.shape, f32),
            jax.ShapeDtypeStruct((devices, send_rows, node_cells), f32),
        ),
        in_specs=[SMEM] * 5 + [VMEM, ANY, ANY, ANY] + [VMEM] * 6,
        out_specs=(VMEM, VMEM, VMEM),
        scratch_shapes=[
            pltpu.VMEM((local_faces + rim_count, lanes), f32),
            pltpu.VMEM((2 * block_faces, lanes), f32),
            pltpu.VMEM((faces, lanes, lanes), f32),
            pltpu.VMEM((blocks, block_faces), f32),
            pltpu.VMEM((blocks, block_faces), f32),
            pltpu.VMEM((blocks, block_faces), f32),
            pltpu.VMEM((high.shape[1], 3 * lanes), f32),
            pltpu.SMEM((devices,), jnp.int32),
            pltpu.SemaphoreType.DMA((3,)),
        ],
        compiler_params=params,
    )(
        own, face_map, wet_blocks, breach, block_plan,
        fields, table, from_before, from_after,
        metric, face_scale, face_angle, face_map, jnp.asarray(high), jnp.asarray(low[:, low_start:]),
    )

    got = lax.all_to_all(send, "mesh", split_axis=0, concat_axis=0, tiled=True)
    slot_ids = own_index * blocks + jnp.arange(blocks, dtype=jnp.int32)
    every_slot = jnp.arange(block_plan.shape[0], dtype=jnp.int32)
    source = jnp.sum(
        jnp.where(block_plan[None, :] == slot_ids[:, None], every_slot[None, :], 0), axis=1
    ) // blocks
    return pl.pallas_call(
        merge_kernel,
        out_shape=(
            jax.ShapeDtypeStruct(water_depth.shape, f32),
            jax.ShapeDtypeStruct(momentum.shape, f32),
        ),
        in_specs=[SMEM, SMEM, VMEM, VMEM, VMEM],
        out_specs=(VMEM, VMEM),
        compiler_params=params,
    )(source, own, got, depth, flow)


def solution(mesh):
    in_specs = (
        P(("groups", "mesh"), None, None),
        P(("groups", "mesh"), None, None, None),
        P(("groups", "mesh"), None, None),
        P(("groups", "mesh"), None),
        P(("groups", "mesh"), None),
        P(("groups", "mesh"), None),
        P(("groups", "mesh"), None),
        P(("groups", "mesh")),
        P(("groups", "mesh"), None),
        P("groups"),
    )
    out_specs = (P(("groups", "mesh"), None, None), P(("groups", "mesh"), None, None, None))
    return jax.shard_map(body, mesh=mesh, in_specs=in_specs, out_specs=out_specs, check_vma=False)
```

profile of v0, /device:TPU:13, one launch (start us, length us, event | category | flops | bytes accessed | tf_op | source)
XLA Modules:
  0.0 77.5 jit_solution(9299324956652189941)
XLA Ops:
  0.6 1.6 %copy.20.refs_1_ = f32[24,2,10,640]{3,2,1,0:T(8,128)S(1)} copy(f32[24,2,10,640]{3,1,2,0:T(2,128)} %param.13) | data formatting | bytes 2457600 | tf_op args[1]
  2.3 0.0 copy-start.12
  2.3 0.0 copy-start.2
  2.3 0.0 copy-start.3
  2.3 0.0 copy-start.4
  2.3 0.0 copy-start.5
  2.3 0.0 copy-start.6
  2.3 0.0 copy-start.7
  2.3 0.0 copy-start.8
  2.4 0.0 copy-start.10
  2.4 0.2 copy.19.refs_0_
  2.5 5.2 %shard_map.131 = (f32[12,3,112,128]{3,2,1,0:T(8,128)S(1)}, f32[4608,128]{1,0:T(8,128)}, f32[128,128]{1,0:T(8,128)S(1)}) custom-call(f32[24,10,640]{2,1,0:T(8,128)S(1)} %copy.19.refs_0_, f32[24,2,10,640]{3,2,1,0:T(8,128)S(1)} %copy.20.refs_1_, s32[1,128]{1,0:T(1,128)S(1)} %copy-done.9), custom_call_target="tpu_custom_call" | custom-call | tf_op jit(solution)/shard_map/pallas_call | solution.py:456
  7.8 1.3 %copy-done = f32[12,3,112,128]{3,2,1,0:T(8,128)} copy-done((f32[12,3,112,128]{3,2,1,0:T(8,128)}, f32[12,3,112,128]{3,2,1,0:T(8,128)S(1)}, u32[]{:S(2)}) %copy-start) | copy-done | bytes 2064408
  9.1 3.7 %collective-permute-start = (f32[64,128]{1,0:T(8,128)S(1)}, f32[64,128]{1,0:T(8,128)S(1)}, u32[]{:S(2)}, u32[]{:S(2)}) collective-permute-start(f32[64,128]{1,0:T(8,128)S(1)} %get-tuple-element.19), channel_id=1, source_target_pairs={{0,1},{1,2},{2,3},{3,4},{4,5},{5,6},{6,7},{7,8},{8,9},{9,10},{10,1... | collective-permute-start | bytes 98312 | tf_op jit(solution)/shard_map/ppermute | solution.py:470
  12.8 1.9 %collective-permute-start.1 = (f32[64,128]{1,0:T(8,128)S(1)}, f32[64,128]{1,0:T(8,128)S(1)}, u32[]{:S(2)}, u32[]{:S(2)}) collective-permute-start(f32[64,128]{1,0:T(8,128)S(1)} %get-tuple-element.18), channel_id=1, source_target_pairs={{1,0},{2,1},{3,2},{4,3},{5,4},{6,5},{7,6},{8,7},{9,8},{10,9},{11,1... | collective-permute-start | bytes 98312 | tf_op jit(solution)/shard_map/ppermute | solution.py:471
  14.7 0.1 copy.21.refs_3_
  14.8 0.0 collective-permute-done.refs_7_
  14.8 4.1 %collective-permute-done.1.refs_8_ = f32[64,128]{1,0:T(8,128)S(1)} collective-permute-done((f32[64,128]{1,0:T(8,128)S(1)}, f32[64,128]{1,0:T(8,128)S(1)}, u32[]{:S(2)}, u32[]{:S(2)}) %collective-permute-start.1) | collective-permute-done | bytes 32800 | tf_op jit(solution)/shard_map/ppermute | solution.py:471
  18.9 0.0 copy-done.4
  18.9 0.0 copy-done.5
  18.9 0.0 copy-done.6
  18.9 0.0 copy-done.7
  19.0 0.0 copy-done.8
  19.0 0.0 copy-done.10
  19.0 16.7 %shard_map.132 = (f32[24,10,640]{2,1,0:T(8,128)S(1)}, f32[24,2,10,640]{3,2,1,0:T(8,128)S(1)}, f32[16,32,640]{2,1,0:T(8,128)}) custom-call(s32[1]{0:T(128)} %bitcast.refs_0_.own_ref, s32[24,192]{1,0:T(8,128)S(1)} %copy-done.2, s32[24]{0:T(128)S(1)} %copy-done.10, s32[24,10]{1,0:T(8,128)S(1)} %copy.21.refs_3_, s32[384]{0:T(512)S(1)} %copy-done.8, ...), custom_call_target="tpu_custom_call" | custom-call | tf_op jit(solution)/shard_map/pallas_call | solution.py:477
  35.7 1.3 %copy-done.1 = f32[24,2,10,640]{3,2,1,0:T(8,128)} copy-done((f32[24,2,10,640]{3,2,1,0:T(8,128)}, f32[24,2,10,640]{3,2,1,0:T(8,128)S(1)}, u32[]{:S(2)}) %copy-start.1) | copy-done | bytes 1228824
  37.0 5.0 %all-to-all-start = ((f32[16,32,640]{2,1,0:T(8,128)}), f32[16,32,640]{2,1,0:T(8,128)S(1)}, u32[]{:S(2)}, u32[]{:S(2)}) async-start(f32[16,32,640]{2,1,0:T(8,128)} %get-tuple-element.11), calls=%async_computation | async-start | bytes 2621440 | tf_op jit(solution)/shard_map/all_to_all | solution.py:504
  42.0 0.2 select_reduce_fusion
  42.2 30.4 %all-to-all-done.got_ref = f32[16,32,640]{2,1,0:T(8,128)S(1)} async-done(((f32[16,32,640]{2,1,0:T(8,128)}), f32[16,32,640]{2,1,0:T(8,128)S(1)}, u32[]{:S(2)}, u32[]{:S(2)}) %all-to-all-start) | async-done | bytes 1310752 | tf_op jit(solution)/shard_map/all_to_all | solution.py:504
  72.5 2.3 %shard_map.133 = (f32[24,10,640]{2,1,0:T(8,128)S(1)}, f32[24,2,10,640]{3,2,1,0:T(8,128)S(1)}) custom-call(s32[24]{0:T(128)S(1)} %and_select_fusion.source_ref, s32[1]{0:T(128)} %bitcast.refs_0_.own_ref, f32[16,32,640]{2,1,0:T(8,128)S(1)} %all-to-all-done.got_ref, f32[24,10,640]{2,1,0:T(8,128)S(1)} %get-tuple-element.12.depth_ref, f32[24,2,10,640]{3,2,1,0:T(8,128)} %copy-done.1), custom_call_target="tpu_custom_call" | custom-call | tf_op jit(solution)/shard_map/pallas_call | solution.py:510
  74.8 1.7 %copy.23 = f32[24,2,10,640]{3,1,2,0:T(2,128)} copy(f32[24,2,10,640]{3,2,1,0:T(8,128)S(1)} %get-tuple-element.17) | data formatting | bytes 2457600 | tf_op jit(solution)/shard_map/pallas_call | solution.py:510
  76.5 1.0 %copy.22 = f32[24,10,640]{2,0,1:T(8,128)} copy(f32[24,10,640]{2,1,0:T(8,128)S(1)} %get-tuple-element.16) | data formatting | bytes 1228800 | tf_op jit(solution)/shard_map/pallas_call | solution.py:510
  (12 shorter events, 0.0 us)
Async XLA Ops:
  0.6 1.6 %copy-start.11 = (f32[24,10,640]{2,0,1:T(8,128)S(1)}, f32[24,10,640]{2,0,1:T(8,128)}, u32[]{:S(2)}) copy-start(f32[24,10,640]{2,0,1:T(8,128)} %param.12) | copy-start | bytes 1843204
  0.6 1.9 %copy-start.9 = (s32[1,128]{1,0:T(1,128)S(1)}, s32[1,128]{1,0:T(1,128)}, u32[]{:S(2)}) copy-start(s32[1,128]{1,0:T(1,128)} %refs_2_.2) | copy-start | bytes 1540
  2.3 12.5 %copy-start.12 = (s32[24,10]{0,1:T(8,128)S(1)}, s32[24,10]{0,1:T(8,128)}, u32[]{:S(2)}) copy-start(s32[24,10]{0,1:T(8,128)} %param.20) | copy-start | bytes 2884
  2.3 16.6 %copy-start.2 = (s32[24,192]{1,0:T(8,128)S(1)}, s32[24,192]{1,0:T(8,128)}, u32[]{:S(2)}) copy-start(s32[24,192]{1,0:T(8,128)} %refs_12_.1) | copy-start | bytes 55300
  2.3 16.6 %copy-start.3 = (bf16[112,352]{1,0:T(8,128)(2,1)S(1)}, bf16[112,352]{1,0:T(8,128)(2,1)}, u32[]{:S(2)}) copy-start(bf16[112,352]{1,0:T(8,128)(2,1)} %constant.20.clone.refs_13_) | copy-start | bytes 236548
  2.3 16.6 %copy-start.4 = (bf16[112,352]{1,0:T(8,128)(2,1)S(1)}, bf16[112,352]{1,0:T(8,128)(2,1)}, u32[]{:S(2)}) copy-start(bf16[112,352]{1,0:T(8,128)(2,1)} %constant.21.clone.refs_14_) | copy-start | bytes 236548
  2.3 16.6 %copy-start.5 = (f32[24,4,64]{2,1,0:T(4,128)S(1)}, f32[24,4,64]{2,1,0:T(4,128)}, u32[]{:S(2)}) copy-start(f32[24,4,64]{2,1,0:T(4,128)} %refs_9_.1) | copy-start | bytes 73732
  2.3 16.6 %copy-start.6 = (f32[24,192]{1,0:T(8,128)S(1)}, f32[24,192]{1,0:T(8,128)}, u32[]{:S(2)}) copy-start(f32[24,192]{1,0:T(8,128)} %refs_10_.1) | copy-start | bytes 55300
  2.3 16.6 %copy-start.7 = (f32[24,192]{1,0:T(8,128)S(1)}, f32[24,192]{1,0:T(8,128)}, u32[]{:S(2)}) copy-start(f32[24,192]{1,0:T(8,128)} %refs_11_.1) | copy-start | bytes 55300
  2.3 16.6 %copy-start.8 = (s32[384]{0:T(512)S(1)}, s32[384]{0:T(512)}, u32[]{:S(2)}) copy-start(s32[384]{0:T(512)} %refs_4_.1) | copy-start | bytes 4612
  2.4 16.6 %copy-start.10 = (s32[24]{0:T(128)S(1)}, s32[24]{0:T(128)}, u32[]{:S(2)}) copy-start(s32[24]{0:T(128)} %refs_2_.3) | copy-start | bytes 292
  7.8 1.3 %copy-start = (f32[12,3,112,128]{3,2,1,0:T(8,128)}, f32[12,3,112,128]{3,2,1,0:T(8,128)S(1)}, u32[]{:S(2)}) copy-start(f32[12,3,112,128]{3,2,1,0:T(8,128)S(1)} %get-tuple-element.8.refs_5_) | copy-start | bytes 6193156
  9.1 5.7 %collective-permute-start = (f32[64,128]{1,0:T(8,128)S(1)}, f32[64,128]{1,0:T(8,128)S(1)}, u32[]{:S(2)}, u32[]{:S(2)}) collective-permute-start(f32[64,128]{1,0:T(8,128)S(1)} %get-tuple-element.19), channel_id=1, source_target_pairs={{0,1},{1,2},{2,3},{3,4},{4,5},{5,6},{6,7},{7,8},{8,9},{9,10},{10,1... | collective-permute-start | bytes 98312 | tf_op jit(solution)/shard_map/ppermute | solution.py:470
  12.8 6.1 %collective-permute-start.1 = (f32[64,128]{1,0:T(8,128)S(1)}, f32[64,128]{1,0:T(8,128)S(1)}, u32[]{:S(2)}, u32[]{:S(2)}) collective-permute-start(f32[64,128]{1,0:T(8,128)S(1)} %get-tuple-element.18), channel_id=1, source_target_pairs={{1,0},{2,1},{3,2},{4,3},{5,4},{6,5},{7,6},{8,7},{9,8},{10,9},{11,1... | collective-permute-start | bytes 98312 | tf_op jit(solution)/shard_map/ppermute | solution.py:471
  35.7 1.3 %copy-start.1 = (f32[24,2,10,640]{3,2,1,0:T(8,128)}, f32[24,2,10,640]{3,2,1,0:T(8,128)S(1)}, u32[]{:S(2)}) copy-start(f32[24,2,10,640]{3,2,1,0:T(8,128)S(1)} %get-tuple-element.13.flow_ref) | copy-start | bytes 3686404
  37.0 35.6 %all-to-all-start = ((f32[16,32,640]{2,1,0:T(8,128)}), f32[16,32,640]{2,1,0:T(8,128)S(1)}, u32[]{:S(2)}, u32[]{:S(2)}) async-start(f32[16,32,640]{2,1,0:T(8,128)} %get-tuple-element.11), calls=%async_computation | async-start | bytes 2621440 | tf_op jit(solution)/shard_map/all_to_all | solution.py:504
where the time goes:
time: 77.8 us; the launch traced here: 77.5 us
  waiting for transfers between devices  34.5 us (44%)
  Pallas kernels  24.2 us (31%)
  starting transfers between devices  10.6 us (14%)
  local copies, waits for them, and re-layouts  7.18 us (9%)
  between operations  0.86 us (1%)
    all_to_all x1, waiting for transfers between devices, body(): got = lax.all_to_all(send, 'mesh', split_axis=0, concat_axis=0, tiled=True)  30.4 us
    pallas_call x1, Pallas kernels, body(): pl.pallas_call(lambda *refs: advance_kernel(face_nodes, node_count, membe...  16.7 us
    pallas_call x1, Pallas kernels, body(): pl.pallas_call(lambda *refs: layout_kernel(face_nodes, node_count, *refs)...  5.21 us
    all_to_all x1, starting transfers between devices, body(): got = lax.all_to_all(send, 'mesh', split_axis=0, concat_axis=0, tiled=True)  4.99 us
    unnamed x29, local copies, waits for them, and re-layouts  4.5 us
    ppermute x1, waiting for transfers between devices, body(): lax.ppermute(edge[:rim], 'mesh', [(i + 1, i) for i in range(ends)])  4.1 us
    ppermute x1, starting transfers between devices, body(): lax.ppermute(edge[rim:], 'mesh', [(i, i + 1) for i in range(ends)])  3.7 us
    pallas_call x2, local copies, waits for them, and re-layouts, body(): pl.pallas_call(merge_kernel, out_shape=(jax.ShapeDtypeStruct(water_depth....  2.67 us
  transfers between devices with their start and end apart: 3, of which 2 were waited for; matrix products, arithmetic and copies ran while one was open for 0% of the time, Pallas kernels for 0%

commit v1 on v0

--- a/solution.py
+++ b/solution.py
@@ -132,8 +132,9 @@
         ]
 
 
-def layout_kernel(
-    face_nodes, node_count, depth_ref, flow_ref, rim_ref, fields_ref, table_ref, edge_ref, stack_ref
+def lay_out(
+    face_nodes, node_count, order_ref, depth_ref, flow_ref, rim_ref,
+    fields_ref, table_ref, edge_ref, stack_ref,
 ):
     blocks, members, node_cells = depth_ref.shape
     elements = node_cells // node_count
@@ -146,17 +147,18 @@
     stack_ref[...] = jnp.zeros_like(stack_ref)
 
     def one_pair(pair, carry):
+        sides = (order_ref[2 * pair], order_ref[2 * pair + 1])
         for comp in range(3):
             fields_ref[pair, comp, used:rows, :] = jnp.ones((rows - used, lanes), jnp.float32)
             for half in range(node_count // 2):
                 for first, size in ((0, full), (full, rest)):
                     cells = (pl.ds(first, size), pl.ds(half * lanes, lanes))
                     if comp == 0:
-                        one = depth_ref[(2 * pair, *cells)]
-                        two = depth_ref[(2 * pair + 1, *cells)]
+                        one = depth_ref[(sides[0], *cells)]
+                        two = depth_ref[(sides[1], *cells)]
                     else:
-                        one = flow_ref[(2 * pair, comp - 1, *cells)]
-                        two = flow_ref[(2 * pair + 1, comp - 1, *cells)]
+                        one = flow_ref[(sides[0], comp - 1, *cells)]
+                        two = flow_ref[(sides[1], comp - 1, *cells)]
                     low = lanes_low(one.shape, elements)
                     base = node_count * first + 2 * half * size
                     fields_ref[pair, comp, base : base + size, :] = jnp.where(
@@ -180,24 +182,25 @@
         return carry
 
     lax.fori_loop(0, blocks // 2, one_pair, 0)
-    rim_count = rim_ref.shape[1]
+    rim_count = rim_ref.shape[0]
 
     def one_group(group, carry):
         for step in range(16):
             face = group * 16 + step
-            edge_ref[pl.ds(face, 1), :] = table_ref[pl.ds(rim_ref[0, face], 1), :]
+            edge_ref[pl.ds(face, 1), :] = table_ref[pl.ds(rim_ref[face], 1), :]
         return carry
 
     lax.fori_loop(0, rim_count // 16, one_group, 0)
 
 
-def advance_kernel(
-    face_nodes, node_count, members, low_start,
-    own_ref, map_ref, wet_ref, breach_ref, plan_ref,
-    fields_ref, table_ref, before_ref, after_ref,
-    metric_ref, scale_ref, angle_ref, links_ref, high_ref, low_ref,
-    depth_out, flow_out, send_ref,
-    pool_ref, picked_ref, inner_ref, cos_ref, sin_ref, wall_ref, right_ref, chosen_ref, sems,
+def section_kernel(
+    face_nodes, node_count, members, low_start, early,
+    order_ref, map_ref, rim_ref, wet_ref, breach_ref, chosen_ref, slot_ref, source_ref,
+    depth_ref, flow_ref, metric_ref, scale_ref, angle_ref, links_ref, high_ref, low_ref,
+    depth_out, flow_out,
+    fields_ref, pool_ref, edge_ref, before_ref, after_ref, picked_ref, inner_ref,
+    cos_ref, sin_ref, wall_ref, right_ref, moved_ref, send_ref, got_ref,
+    rim_sems, send_sems, got_sems,
 ):
     blocks = depth_out.shape[0]
     elements = metric_ref.shape[2]
@@ -209,13 +212,41 @@
     block_faces = faces * elements
     local_faces = blocks * block_faces
     rim = before_ref.shape[0]
-    copies = [
-        pltpu.make_async_copy(table_ref, pool_ref.at[pl.ds(0, local_faces)], sems.at[0]),
-        pltpu.make_async_copy(before_ref, pool_ref.at[pl.ds(local_faces, rim)], sems.at[1]),
-        pltpu.make_async_copy(after_ref, pool_ref.at[pl.ds(local_faces + rim, rim)], sems.at[2]),
-    ]
-    for copy in copies:
-        copy.start()
+    devices = got_ref.shape[0]
+    own = lax.axis_index("mesh")
+    mesh_type = pl.DeviceIdType.MESH
+
+    barrier = pltpu.get_barrier_semaphore()
+    for step in range(1, devices):
+        pl.semaphore_signal(
+            barrier, inc=1, device_id={"mesh": lax.rem(own + step, devices)},
+            device_id_type=mesh_type,
+        )
+
+    lay_out(
+        face_nodes, node_count, order_ref, depth_ref, flow_ref, rim_ref,
+        fields_ref, pool_ref, edge_ref, inner_ref,
+    )
+    pl.semaphore_wait(barrier, devices - 1)
+
+    to_next = pltpu.make_async_remote_copy(
+        src_ref=edge_ref.at[pl.ds(rim, rim)], dst_ref=before_ref,
+        send_sem=rim_sems.at[0], recv_sem=rim_sems.at[1],
+        device_id={"mesh": lax.rem(own + 1, devices)}, device_id_type=mesh_type,
+    )
+    to_before = pltpu.make_async_remote_copy(
+        src_ref=edge_ref.at[pl.ds(0, rim)], dst_ref=after_ref,
+        send_sem=rim_sems.at[2], recv_sem=rim_sems.at[3],
+        device_id={"mesh": lax.rem(own + devices - 1, devices)}, device_id_type=mesh_type,
+    )
+
+    @pl.when(own < devices - 1)
+    def _():
+        to_next.start()
+
+    @pl.when(own > 0)
+    def _():
+        to_before.start()
 
     angles = angle_ref[...]
     cos_ref[...] = jnp.cos(angles)
@@ -226,38 +257,30 @@
     )
     wall_ref[...] = jnp.where(links_ref[...] == own_number, 1.0, 0.0)
     right_ref[...] = jnp.zeros_like(right_ref)
-
-    own = own_ref[0]
-
-    def clear(index, carry):
-        chosen_ref[index] = 0
-        return carry
-
-    lax.fori_loop(0, chosen_ref.shape[0], clear, 0)
-
-    def choose(index, carry):
-        target = plan_ref[own * blocks + index] // blocks
-
-        @pl.when(target != own)
-        def _():
-            chosen_ref[target] = index
-
-        return carry
-
-    lax.fori_loop(0, blocks, choose, 0)
-    for copy in copies:
-        copy.wait()
+    moved_ref[...] = jnp.zeros_like(moved_ref)
+    got_ref[own] = jnp.zeros(got_ref.shape[1:], jnp.float32)
+
+    @pl.when(own > 0)
+    def _():
+        to_next.wait_recv()
+        pool_ref[local_faces : local_faces + rim, :] = before_ref[...]
+
+    @pl.when(own < devices - 1)
+    def _():
+        to_before.wait_recv()
+        pool_ref[local_faces + rim : local_faces + 2 * rim, :] = after_ref[...]
 
     def one_pair(pair, carry):
+        sides = (order_ref[2 * pair], order_ref[2 * pair + 1])
         for side in range(2):
             for face in range(block_faces):
                 picked_ref[side * block_faces + face : side * block_faces + face + 1, :] = pool_ref[
-                    pl.ds(map_ref[2 * pair + side, face], 1), :
+                    pl.ds(map_ref[sides[side], face], 1), :
                 ]
 
         def face_row(ref, face):
-            first = ref[pl.ds(2 * pair, 1), :]
-            second = ref[pl.ds(2 * pair + 1, 1), :]
+            first = ref[pl.ds(sides[0], 1), :]
+            second = ref[pl.ds(sides[1], 1), :]
             cells = slice(face * elements, (face + 1) * elements)
             return jnp.concatenate([first[:, cells], second[:, cells]], axis=1)
 
@@ -309,7 +332,7 @@
                     half_scale * jumps[comp]
                 )
 
-        factors = jnp.concatenate([metric_ref[2 * pair], metric_ref[2 * pair + 1]], axis=1)
+        factors = jnp.concatenate([metric_ref[sides[0]], metric_ref[sides[1]]], axis=1)
         height = fields_ref[pair, 0]
         flow_x = fields_ref[pair, 1]
         flow_y = fields_ref[pair, 2]
@@ -339,14 +362,14 @@
         )
         row_low = lanes_low((1, lanes), elements)
         step = time_step * jnp.where(
-            row_low, wet_ref[2 * pair].astype(jnp.float32), wet_ref[2 * pair + 1].astype(jnp.float32)
+            row_low, wet_ref[sides[0]].astype(jnp.float32), wet_ref[sides[1]].astype(jnp.float32)
         )
 
         def inflow(member):
             return breach_rate * jnp.where(
                 row_low,
-                breach_ref[2 * pair, member].astype(jnp.float32),
-                breach_ref[2 * pair + 1, member].astype(jnp.float32),
+                breach_ref[sides[0], member].astype(jnp.float32),
+                breach_ref[sides[1], member].astype(jnp.float32),
             )
 
         def inflow_rows(first, size):
@@ -371,59 +394,69 @@
                         both.append(fields_ref[pair, comp, base : base + size, :] + step * change)
                     one = jnp.where(low, both[0], pltpu.roll(both[1], elements, 1))
                     two = jnp.where(low, pltpu.roll(both[0], elements, 1), both[1])
-                    cells = (pl.ds(first, size), pl.ds(half * lanes, lanes))
-                    if comp == 0:
-                        depth_out[(2 * pair, *cells)] = one
-                        depth_out[(2 * pair + 1, *cells)] = two
-                    else:
-                        flow_out[(2 * pair, comp - 1, *cells)] = one
-                        flow_out[(2 * pair + 1, comp - 1, *cells)] = two
+                    base = 3 * first + comp * size
+                    span_out = slice(half * lanes, (half + 1) * lanes)
+                    moved_ref[2 * pair, base : base + size, span_out] = one
+                    moved_ref[2 * pair + 1, base : base + size, span_out] = two
         return carry
 
-    lax.fori_loop(0, blocks // 2, one_pair, 0)
+
+    lax.fori_loop(0, early, one_pair, 0)
 
     def one_send(device, carry):
-        block = chosen_ref[device]
+        send_ref[device] = moved_ref[chosen_ref[device]]
+        return carry
+
+    lax.fori_loop(0, devices, one_send, 0)
+    sends = []
+    for step in sorted(range(1, devices), key=lambda step: abs(step - devices // 2)):
+        target = lax.rem(own + step, devices)
+        sends.append(
+            pltpu.make_async_remote_copy(
+                src_ref=send_ref.at[target], dst_ref=got_ref.at[own],
+                send_sem=send_sems.at[target], recv_sem=got_sems.at[own],
+                device_id={"mesh": target}, device_id_type=mesh_type,
+            )
+        )
+    for copy in sends:
+        copy.start()
+
+    lax.fori_loop(early, blocks // 2, one_pair, 0)
+
+    for step in range(1, devices):
+        origin = lax.rem(own + step, devices)
+        pltpu.make_async_remote_copy(
+            src_ref=send_ref.at[origin], dst_ref=got_ref.at[origin],
+            send_sem=send_sems.at[origin], recv_sem=got_sems.at[origin],
+            device_id={"mesh": origin}, device_id_type=mesh_type,
+        ).wait_recv()
+
+    def one_slot(slot, carry):
+        stays = source_ref[slot] == own
         for comp in range(3):
             for first, size in ((0, full), (full, rest)):
                 base = 3 * first + comp * size
+                span = slice(base, base + size)
+                value = jnp.where(
+                    stays, moved_ref[slot_ref[slot], span, :], got_ref[source_ref[slot], span, :]
+                )
                 if comp == 0:
-                    value = depth_out[block, first : first + size, :]
+                    depth_out[slot, first : first + size, :] = value
                 else:
-                    value = flow_out[block, comp - 1, first : first + size, :]
-                send_ref[device, base : base + size, :] = value
+                    flow_out[slot, comp - 1, first : first + size, :] = value
         return carry
 
-    lax.fori_loop(0, send_ref.shape[0], one_send, 0)
-
-
-def merge_kernel(source_ref, own_ref, got_ref, depth_ref, flow_ref, depth_out, flow_out):
-    blocks, members, _ = depth_ref.shape
-    full = members // 8 * 8
-    rest = members - full
-
-    def one_slot(slot, carry):
-        source = source_ref[slot]
-
-        @pl.when(source == own_ref[0])
-        def _():
-            depth_out[slot] = depth_ref[slot]
-            flow_out[slot] = flow_ref[slot]
-
-        @pl.when(source != own_ref[0])
-        def _():
-            for comp in range(3):
-                for first, size in ((0, full), (full, rest)):
-                    base = 3 * first + comp * size
-                    value = got_ref[source, base : base + size, :]
-                    if comp == 0:
-                        depth_out[slot, first : first + size, :] = value
-                    else:
-                        flow_out[slot, comp - 1, first : first + size, :] = value
-
-        return carry
-
     lax.fori_loop(0, blocks, one_slot, 0)
+    for copy in sends:
+        copy.wait_send()
+
+    @pl.when(own < devices - 1)
+    def _():
+        to_next.wait_send()
+
+    @pl.when(own > 0)
+    def _():
+        to_before.wait_send()
 
 
 def body(
@@ -448,75 +481,74 @@
     local_faces = blocks * block_faces
     rim_count = rim_faces.shape[1]
     rim = rim_count // 2
-    own_index = lax.axis_index("mesh")
+    own = lax.axis_index("mesh").astype(jnp.int32)
     devices = lax.axis_size("mesh")
-    params = pltpu.CompilerParams(vmem_limit_bytes=48 * 2**20)
     f32 = jnp.float32
 
-    fields, table, edge = pl.pallas_call(
-        lambda *refs: layout_kernel(face_nodes, node_count, *refs),
-        out_shape=(
-            jax.ShapeDtypeStruct((blocks // 2, 3, rows, lanes), f32),
-            jax.ShapeDtypeStruct((local_faces, lanes), f32),
-            jax.ShapeDtypeStruct((rim_count, lanes), f32),
-        ),
-        in_specs=[VMEM, VMEM, SMEM],
-        out_specs=(VMEM, VMEM, VMEM),
-        scratch_shapes=[pltpu.VMEM((faces, lanes, lanes), f32)],
-        compiler_params=params,
-    )(water_depth, momentum, rim_faces)
-
-    ends = devices - 1
-    from_before = lax.ppermute(edge[rim:], "mesh", [(i, i + 1) for i in range(ends)])
-    from_after = lax.ppermute(edge[:rim], "mesh", [(i + 1, i) for i in range(ends)])
+    local_ids = jnp.arange(blocks, dtype=jnp.int32)
+    targets = lax.dynamic_slice_in_dim(block_plan, own * blocks, blocks) // blocks
+    stays = (targets == own).astype(jnp.int32)
+    keys = stays * blocks + local_ids
+    place = jnp.sum((keys[None, :] < keys[:, None]).astype(jnp.int32), axis=1)
+    order = jnp.sum(jnp.where(place[None, :] == local_ids[:, None], local_ids[None, :], 0), axis=1)
+    device_ids = jnp.arange(devices, dtype=jnp.int32)
+    chosen = jnp.sum(jnp.where(targets[None, :] == device_ids[:, None], place[None, :], 0), axis=1)
+    chosen = jnp.where(device_ids == own, 0, chosen)
+    slot_ids = own * blocks + local_ids
+    every_slot = jnp.arange(block_plan.shape[0], dtype=jnp.int32)
+    source = jnp.sum(
+        jnp.where(block_plan[None, :] == slot_ids[:, None], every_slot[None, :], 0), axis=1
+    )
+    origin = jnp.clip(source - own * blocks, 0, blocks - 1)
+    slot_place = jnp.sum(jnp.where(origin[:, None] == local_ids[None, :], place[None, :], 0), axis=1)
+    source = source // blocks
+
+    def to_place(numbers):
+        block = numbers // block_faces
+        shift = jnp.zeros_like(numbers)
+        for index in range(blocks):
+            shift = jnp.where(block == index, (place[index] - index) * block_faces, shift)
+        return numbers + shift
 
     high, low = combined_matrix(members, rows, node_count)
     low_start = 2 * rows if not np.any(low[:, : 2 * rows].astype(np.float32)) else 0
-    own = jnp.reshape(own_index.astype(jnp.int32), (1,))
+    early = min(-(-(devices // 2) // 2), blocks // 2)
     send_rows = round_up(3 * members, 8)
-    depth, flow, send = pl.pallas_call(
-        lambda *refs: advance_kernel(face_nodes, node_count, members, low_start, *refs),
+    return pl.pallas_call(
+        lambda *refs: section_kernel(face_nodes, node_count, members, low_start, early, *refs),
         out_shape=(
             jax.ShapeDtypeStruct(water_depth.shape, f32),
             jax.ShapeDtypeStruct(momentum.shape, f32),
-            jax.ShapeDtypeStruct((devices, send_rows, node_cells), f32),
         ),
-        in_specs=[SMEM] * 5 + [VMEM, ANY, ANY, ANY] + [VMEM] * 6,
-        out_specs=(VMEM, VMEM, VMEM),
+        in_specs=[SMEM] * 8 + [VMEM] * 8,
+        out_specs=(VMEM, VMEM),
         scratch_shapes=[
+            pltpu.VMEM((blocks // 2, 3, rows, lanes), f32),
             pltpu.VMEM((local_faces + rim_count, lanes), f32),
+            pltpu.VMEM((rim_count, lanes), f32),
+            pltpu.VMEM((rim, lanes), f32),
+            pltpu.VMEM((rim, lanes), f32),
             pltpu.VMEM((2 * block_faces, lanes), f32),
             pltpu.VMEM((faces, lanes, lanes), f32),
             pltpu.VMEM((blocks, block_faces), f32),
             pltpu.VMEM((blocks, block_faces), f32),
             pltpu.VMEM((blocks, block_faces), f32),
             pltpu.VMEM((high.shape[1], 3 * lanes), f32),
-            pltpu.SMEM((devices,), jnp.int32),
-            pltpu.SemaphoreType.DMA((3,)),
+            pltpu.VMEM((blocks, send_rows, node_cells), f32),
+            pltpu.VMEM((devices, send_rows, node_cells), f32),
+            pltpu.VMEM((devices, send_rows, node_cells), f32),
+            pltpu.SemaphoreType.DMA((4,)),
+            pltpu.SemaphoreType.DMA((devices,)),
+            pltpu.SemaphoreType.DMA((devices,)),
         ],
-        compiler_params=params,
+        compiler_params=pltpu.CompilerParams(
+            vmem_limit_bytes=48 * 2**20, collective_id=0, has_side_effects=True
+        ),
     )(
-        own, face_map, wet_blocks, breach, block_plan,
-        fields, table, from_before, from_after,
-        metric, face_scale, face_angle, face_map, jnp.asarray(high), jnp.asarray(low[:, low_start:]),
-    )
-
-    got = lax.all_to_all(send, "mesh", split_axis=0, concat_axis=0, tiled=True)
-    slot_ids = own_index * blocks + jnp.arange(blocks, dtype=jnp.int32)
-    every_slot = jnp.arange(block_plan.shape[0], dtype=jnp.int32)
-    source = jnp.sum(
-        jnp.where(block_plan[None, :] == slot_ids[:, None], every_slot[None, :], 0), axis=1
-    ) // blocks
-    return pl.pallas_call(
-        merge_kernel,
-        out_shape=(
-            jax.ShapeDtypeStruct(water_depth.shape, f32),
-            jax.ShapeDtypeStruct(momentum.shape, f32),
-        ),
-        in_specs=[SMEM, SMEM, VMEM, VMEM, VMEM],
-        out_specs=(VMEM, VMEM),
-        compiler_params=params,
-    )(source, own, got, depth, flow)
+        order, to_place(face_map), to_place(rim_faces.reshape(-1)), wet_blocks, breach, chosen,
+        slot_place, source, water_depth, momentum, metric, face_scale, face_angle, face_map,
+        jnp.asarray(high), jnp.asarray(low[:, low_start:]),
+    )
 
 
 def solution(mesh):

time: 77.8 us -> 71.8 us (0.923)
  waiting for transfers between devices: 34.5 us -> 0 us
  Pallas kernels: 24.2 us -> 44 us
  between operations: 0.86 us -> 15.8 us
  starting transfers between devices: 10.6 us -> 0 us
  other arithmetic: 0.2 us -> 3.73 us
    all_to_all x1 -> x0, waiting for transfers between devices: 30.4 us -> none  [body(): got = lax.all_to_all(send, 'mesh', split_axis=0, concat_axis=0, tiled=True)]
    pallas_call x3 -> x1, Pallas kernels: 24.2 us -> 44 us  [body(): pl.pallas_call(lambda *refs: section_kernel(face_nodes, node_count, membe...]
    ppermute x2 -> x0, starting transfers between devices: 5.62 us -> none  [the longest x1 3.7 us: body(): lax.ppermute(edge[rim:], 'mesh', [(i, i + 1) for i in range(ends)])]
    all_to_all x1 -> x0, starting transfers between devices: 4.99 us -> none  [body(): got = lax.all_to_all(send, 'mesh', split_axis=0, concat_axis=0, tiled=True)]
    ppermute x2 -> x0, waiting for transfers between devices: 4.11 us -> none  [the longest x1 4.1 us: body(): lax.ppermute(edge[:rim], 'mesh', [(i + 1, i) for i in range(ends)])]
    add x1 -> x4, other arithmetic: 0.01 us -> 2.28 us  [the longest x2 1.51 us: to_place(): return numbers + shift]
    slice x1 -> x2, local copies, waits for them, and re-layouts: 0.01 us -> 1.42 us  [to_place(): place[index] - index]
    unnamed x29 -> x19, local copies, waits for them, and re-layouts: 4.5 us -> 3.58 us
  transfers between devices with their start and end apart: 3 -> 0, of which waited for: 2 -> 0; matrix products, arithmetic and copies ran while one was open for 0% -> 0% of each run, Pallas kernels for 0% -> 0%
where the time goes in v1:
time: 71.8 us; the launch traced here: 71.2 us
  Pallas kernels  44 us (61%)
  between operations  15.8 us (22%)
  local copies, waits for them, and re-layouts  7.67 us (11%)
  other arithmetic  3.73 us (5%)
    pallas_call x1, Pallas kernels, body(): pl.pallas_call(lambda *refs: section_kernel(face_nodes, node_count, membe...  44 us
    unnamed x19, local copies, waits for them, and re-layouts  3.58 us
    pallas_call x2, local copies, waits for them, and re-layouts, body(): pl.pallas_call(lambda *refs: section_kernel(face_nodes, node_count, membe...  2.67 us
    add x2, other arithmetic, to_place(): return numbers + shift  1.51 us

profile of v1, /device:TPU:13, one launch (start us, length us, event | category | flops | bytes accessed | tf_op | source)
XLA Modules:
  0.0 71.2 jit_solution(28132865487614991)
XLA Ops:
  0.6 0.0 copy-start.7
  0.7 1.0 %select_reduce_fusion = s32[24]{0:T(128)S(1)} fusion(s32[384]{0:T(512)} %param.21, s32[24]{0:T(128)S(1)} %iota_add_fusion), kind=kLoop, calls=%fused_computation.1 | loop fusion | flops 27624 | bytes 1728 | tf_op jit(solution)/shard_map/reduce_sum | solution.py:499
  1.6 0.8 %fusion.1 = (s32[24]{0:T(128)S(1)}, s32[24]{0:T(128)S(1)}) fusion(s32[]{:T(128)S(6)} %axis_index.12, s32[384]{0:T(512)} %param.21, s32[]{:T(128)S(6)} %select_n.186), kind=kLoop, calls=%fused_computation.42 | loop fusion | flops 264 | bytes 296 | tf_op jit(solution)/shard_map/add | solution.py:491
  2.4 0.2 convert_reduce_fusion
  2.6 0.1 select_reduce_fusion.3
  2.7 0.2 select_reduce_fusion.1
  2.9 0.7 fusion.4
  6.8 0.7 %fusion.3 = (s32[1]{0:T(128)}, s32[1]{0:T(128)}, s32[1]{0:T(128)}, s32[1]{0:T(128)}, s32[1]{0:T(128)}, /*index=5*/s32[1]{0:T(128)}, s32[1]{0:T(128)}, s32[1]{0:T...) fusion(s32[24]{0:T(128)S(1)} %convert_reduce_fusion), kind=kLoop, calls=%fused_computation.48 | loop fusion | bytes 152 | tf_op jit(solution)/shard_map/slice | solution.py:510
  19.4 0.7 fusion.2.refs_2_
  20.1 0.8 %select_add_fusion.refs_1_ = s32[24,192]{1,0:T(8,128)S(1)} fusion(s32[24,192]{1,0:T(8,128)} %refs_13_.1, s32[]{:T(128)} %bitcast.23, s32[]{:T(128)} %bitcast.22, s32[]{:T(128)} %bitcast.21, s32[]{:T(128)} %bitcast.20, s32[]{:T(128)} %bitcast.19, s32[]{:T(128)} %bitcast.18, s32[]{:T(128)} %bitcast.17, s32[]{:T(128)} %bitcast.16, s32[]{:T(128)} %bitcast.15, ...), kind=kLoop, calls=%fused_computation.2 | loop fusion | flops 262656 | bytes 36960 | tf_op jit(solution)/shard_map/add | solution.py:511
  20.9 0.8 %copy.19.refs_4_ = s32[24,10]{1,0:T(8,128)S(1)} copy(s32[24,10]{0,1:T(8,128)} %param.20) | data formatting | bytes 1920 | tf_op args[8]
  21.7 1.2 %copy.20.refs_8_ = f32[24,10,640]{2,1,0:T(8,128)S(1)} copy(f32[24,10,640]{2,0,1:T(8,128)} %param.12) | data formatting | bytes 1228800 | tf_op args[0]
  22.9 0.0 copy-done.7
  22.9 0.0 copy-start
  22.9 0.0 copy-start.1
  22.9 0.0 copy-start.2
  22.9 0.0 copy-start.3
  23.0 0.0 copy-start.4
  23.0 0.0 copy-start.5
  23.0 0.0 copy-start.6
  23.0 1.5 %copy.21.refs_9_ = f32[24,2,10,640]{3,2,1,0:T(8,128)} copy(f32[24,2,10,640]{3,1,2,0:T(2,128)S(1)} %copy-done.7) | data formatting | bytes 2457600 | tf_op args[1]
  24.5 0.0 copy-done
  24.5 0.0 copy-done.1
  24.5 0.0 copy-done.2
  24.5 0.0 copy-done.3
  24.5 0.0 copy-done.4
  24.5 0.0 copy-done.5
  24.5 0.0 copy-done.6
  24.6 44.0 %shard_map.131 = (f32[24,10,640]{2,1,0:T(8,128)S(1)}, f32[24,2,10,640]{3,2,1,0:T(8,128)S(1)}) custom-call(s32[24]{0:T(128)S(1)} %get-tuple-element.7.refs_0_, s32[24,192]{1,0:T(8,128)S(1)} %select_add_fusion.refs_1_, s32[128]{0:T(128)S(1)} %fusion.2.refs_2_, s32[24]{0:T(128)S(1)} %copy-done.6, s32[24,10]{1,0:T(8,128)S(1)} %copy.19.refs_4_, ...), custom_call_target="tpu_custom_call" | custom-call | tf_op jit(solution)/shard_map/pallas_call | solution.py:517
  68.5 1.0 %copy.22 = f32[24,10,640]{2,0,1:T(8,128)} copy(f32[24,10,640]{2,1,0:T(8,128)S(1)} %get-tuple-element.4) | data formatting | bytes 1228800 | tf_op jit(solution)/shard_map/pallas_call | solution.py:517
  69.5 1.7 %copy.23 = f32[24,2,10,640]{3,1,2,0:T(2,128)} copy(f32[24,2,10,640]{3,2,1,0:T(8,128)S(1)} %get-tuple-element.5) | data formatting | bytes 2457600 | tf_op jit(solution)/shard_map/pallas_call | solution.py:517
  (3 shorter events, 0.0 us)
Async XLA Ops:
  0.6 22.3 %copy-start.7 = (f32[24,2,10,640]{3,1,2,0:T(2,128)S(1)}, f32[24,2,10,640]{3,1,2,0:T(2,128)}, u32[]{:S(2)}) copy-start(f32[24,2,10,640]{3,1,2,0:T(2,128)} %param.13) | copy-start | bytes 3686404
  22.9 1.6 %copy-start = (s32[24,192]{1,0:T(8,128)S(1)}, s32[24,192]{1,0:T(8,128)}, u32[]{:S(2)}) copy-start(s32[24,192]{1,0:T(8,128)} %refs_13_.1) | copy-start | bytes 55300
  22.9 1.6 %copy-start.1 = (bf16[112,352]{1,0:T(8,128)(2,1)S(1)}, bf16[112,352]{1,0:T(8,128)(2,1)}, u32[]{:S(2)}) copy-start(bf16[112,352]{1,0:T(8,128)(2,1)} %constant.228.clone.refs_15_) | copy-start | bytes 236548
  22.9 1.6 %copy-start.2 = (bf16[112,352]{1,0:T(8,128)(2,1)S(1)}, bf16[112,352]{1,0:T(8,128)(2,1)}, u32[]{:S(2)}) copy-start(bf16[112,352]{1,0:T(8,128)(2,1)} %constant.227.clone.refs_14_) | copy-start | bytes 236548
  22.9 1.6 %copy-start.3 = (f32[24,4,64]{2,1,0:T(4,128)S(1)}, f32[24,4,64]{2,1,0:T(4,128)}, u32[]{:S(2)}) copy-start(f32[24,4,64]{2,1,0:T(4,128)} %refs_10_.1) | copy-start | bytes 73732
  23.0 1.6 %copy-start.4 = (f32[24,192]{1,0:T(8,128)S(1)}, f32[24,192]{1,0:T(8,128)}, u32[]{:S(2)}) copy-start(f32[24,192]{1,0:T(8,128)} %refs_11_.1) | copy-start | bytes 55300
  23.0 1.6 %copy-start.5 = (f32[24,192]{1,0:T(8,128)S(1)}, f32[24,192]{1,0:T(8,128)}, u32[]{:S(2)}) copy-start(f32[24,192]{1,0:T(8,128)} %refs_12_.1) | copy-start | bytes 55300
  23.0 1.6 %copy-start.6 = (s32[24]{0:T(128)S(1)}, s32[24]{0:T(128)}, u32[]{:S(2)}) copy-start(s32[24]{0:T(128)} %refs_3_.1) | copy-start | bytes 292

commit v2 on v1

--- a/solution.py
+++ b/solution.py
@@ -133,7 +133,7 @@
 
 
 def lay_out(
-    face_nodes, node_count, order_ref, depth_ref, flow_ref, rim_ref,
+    face_nodes, node_count, order_ref, place_ref, depth_ref, flow_ref, rim_ref,
     fields_ref, table_ref, edge_ref, stack_ref,
 ):
     blocks, members, node_cells = depth_ref.shape
@@ -182,12 +182,16 @@
         return carry
 
     lax.fori_loop(0, blocks // 2, one_pair, 0)
-    rim_count = rim_ref.shape[0]
+    rim_count = rim_ref.shape[1]
+    block_faces = faces * elements
 
     def one_group(group, carry):
         for step in range(16):
             face = group * 16 + step
-            edge_ref[pl.ds(face, 1), :] = table_ref[pl.ds(rim_ref[face], 1), :]
+            number = rim_ref[0, face]
+            block = number // block_faces
+            number = number + (place_ref[block] - block) * block_faces
+            edge_ref[pl.ds(face, 1), :] = table_ref[pl.ds(number, 1), :]
         return carry
 
     lax.fori_loop(0, rim_count // 16, one_group, 0)
@@ -195,7 +199,7 @@
 
 def section_kernel(
     face_nodes, node_count, members, low_start, early,
-    order_ref, map_ref, rim_ref, wet_ref, breach_ref, chosen_ref, slot_ref, source_ref,
+    order_ref, place_ref, map_ref, rim_ref, wet_ref, breach_ref, chosen_ref, slot_ref, source_ref,
     depth_ref, flow_ref, metric_ref, scale_ref, angle_ref, links_ref, high_ref, low_ref,
     depth_out, flow_out,
     fields_ref, pool_ref, edge_ref, before_ref, after_ref, picked_ref, inner_ref,
@@ -209,6 +213,7 @@
     full = members // 8 * 8
     rest = members - full
     face_rows = face_points * members
+    halves = node_count // 2
     block_faces = faces * elements
     local_faces = blocks * block_faces
     rim = before_ref.shape[0]
@@ -224,7 +229,7 @@
         )
 
     lay_out(
-        face_nodes, node_count, order_ref, depth_ref, flow_ref, rim_ref,
+        face_nodes, node_count, order_ref, place_ref, depth_ref, flow_ref, rim_ref,
         fields_ref, pool_ref, edge_ref, inner_ref,
     )
     pl.semaphore_wait(barrier, devices - 1)
@@ -260,6 +265,32 @@
     moved_ref[...] = jnp.zeros_like(moved_ref)
     got_ref[own] = jnp.zeros(got_ref.shape[1:], jnp.float32)
 
+    def volume(pair, right_ref):
+        sides = (order_ref[2 * pair], order_ref[2 * pair + 1])
+        factors = jnp.concatenate([metric_ref[sides[0]], metric_ref[sides[1]]], axis=1)
+        height = fields_ref[pair, 0]
+        flow_x = fields_ref[pair, 1]
+        flow_y = fields_ref[pair, 2]
+        inverse = 1.0 / height
+        pressure = 0.5 * gravity * height * height
+        speed_x = flow_x * inverse
+        speed_y = flow_y * inverse
+        cross = flow_x * speed_y
+        flux_f = (flow_x, flow_x * speed_x + pressure, cross)
+        flux_g = (flow_y, cross, flow_y * speed_y + pressure)
+        for comp in range(3):
+            span = slice(comp * lanes, (comp + 1) * lanes)
+            right_ref[0:rows, span] = factors[0:1] * flux_f[comp] + factors[2:3] * flux_g[comp]
+            right_ref[rows : 2 * rows, span] = (
+                factors[1:2] * flux_f[comp] + factors[3:4] * flux_g[comp]
+            )
+
+    def early_volume(pair, carry):
+        volume(pair, right_ref.at[pair])
+        return carry
+
+    lax.fori_loop(0, early, early_volume, 0)
+
     @pl.when(own > 0)
     def _():
         to_next.wait_recv()
@@ -270,7 +301,7 @@
         to_before.wait_recv()
         pool_ref[local_faces + rim : local_faces + 2 * rim, :] = after_ref[...]
 
-    def one_pair(pair, carry):
+    def one_pair(pair, right_ref):
         sides = (order_ref[2 * pair], order_ref[2 * pair + 1])
         for side in range(2):
             for face in range(block_faces):
@@ -332,23 +363,6 @@
                     half_scale * jumps[comp]
                 )
 
-        factors = jnp.concatenate([metric_ref[sides[0]], metric_ref[sides[1]]], axis=1)
-        height = fields_ref[pair, 0]
-        flow_x = fields_ref[pair, 1]
-        flow_y = fields_ref[pair, 2]
-        inverse = 1.0 / height
-        pressure = 0.5 * gravity * height * height
-        speed_x = flow_x * inverse
-        speed_y = flow_y * inverse
-        cross = flow_x * speed_y
-        flux_f = (flow_x, flow_x * speed_x + pressure, cross)
-        flux_g = (flow_y, cross, flow_y * speed_y + pressure)
-        for comp in range(3):
-            span = slice(comp * lanes, (comp + 1) * lanes)
-            right_ref[0:rows, span] = factors[0:1] * flux_f[comp] + factors[2:3] * flux_g[comp]
-            right_ref[rows : 2 * rows, span] = (
-                factors[1:2] * flux_f[comp] + factors[3:4] * flux_g[comp]
-            )
         right = right_ref[...]
         right_high = right.astype(jnp.bfloat16)
         right_low = (right - right_high.astype(jnp.float32)).astype(jnp.bfloat16)
@@ -368,8 +382,8 @@
         def inflow(member):
             return breach_rate * jnp.where(
                 row_low,
-                breach_ref[sides[0], member].astype(jnp.float32),
-                breach_ref[sides[1], member].astype(jnp.float32),
+                breach_ref[member, sides[0]].astype(jnp.float32),
+                breach_ref[member, sides[1]].astype(jnp.float32),
             )
 
         def inflow_rows(first, size):
@@ -394,14 +408,21 @@
                         both.append(fields_ref[pair, comp, base : base + size, :] + step * change)
                     one = jnp.where(low, both[0], pltpu.roll(both[1], elements, 1))
                     two = jnp.where(low, pltpu.roll(both[0], elements, 1), both[1])
-                    base = 3 * first + comp * size
-                    span_out = slice(half * lanes, (half + 1) * lanes)
-                    moved_ref[2 * pair, base : base + size, span_out] = one
-                    moved_ref[2 * pair + 1, base : base + size, span_out] = two
-        return carry
-
-
-    lax.fori_loop(0, early, one_pair, 0)
+                    base = halves * 3 * first + (comp * halves + half) * size
+                    moved_ref[2 * pair, base : base + size, :] = one
+                    moved_ref[2 * pair + 1, base : base + size, :] = two
+
+
+    def early_pair(pair, carry):
+        one_pair(pair, right_ref.at[pair])
+        return carry
+
+    def late_pair(pair, carry):
+        volume(pair, right_ref.at[0])
+        one_pair(pair, right_ref.at[0])
+        return carry
+
+    lax.fori_loop(0, early, early_pair, 0)
 
     def one_send(device, carry):
         send_ref[device] = moved_ref[chosen_ref[device]]
@@ -421,7 +442,7 @@
     for copy in sends:
         copy.start()
 
-    lax.fori_loop(early, blocks // 2, one_pair, 0)
+    lax.fori_loop(early, blocks // 2, late_pair, 0)
 
     for step in range(1, devices):
         origin = lax.rem(own + step, devices)
@@ -433,17 +454,17 @@
 
     def one_slot(slot, carry):
         stays = source_ref[slot] == own
+        block = jnp.where(stays, moved_ref[slot_ref[slot]], got_ref[source_ref[slot]])
         for comp in range(3):
-            for first, size in ((0, full), (full, rest)):
-                base = 3 * first + comp * size
-                span = slice(base, base + size)
-                value = jnp.where(
-                    stays, moved_ref[slot_ref[slot], span, :], got_ref[source_ref[slot], span, :]
-                )
-                if comp == 0:
-                    depth_out[slot, first : first + size, :] = value
-                else:
-                    flow_out[slot, comp - 1, first : first + size, :] = value
+            for half in range(halves):
+                for first, size in ((0, full), (full, rest)):
+                    base = halves * 3 * first + (comp * halves + half) * size
+                    value = block[base : base + size]
+                    cells = (slice(first, first + size), slice(half * lanes, (half + 1) * lanes))
+                    if comp == 0:
+                        depth_out[(slot, *cells)] = value
+                    else:
+                        flow_out[(slot, comp - 1, *cells)] = value
         return carry
 
     lax.fori_loop(0, blocks, one_slot, 0)
@@ -503,24 +524,23 @@
     slot_place = jnp.sum(jnp.where(origin[:, None] == local_ids[None, :], place[None, :], 0), axis=1)
     source = source // blocks
 
-    def to_place(numbers):
-        block = numbers // block_faces
-        shift = jnp.zeros_like(numbers)
-        for index in range(blocks):
-            shift = jnp.where(block == index, (place[index] - index) * block_faces, shift)
-        return numbers + shift
+    owner = face_map // block_faces
+    shifts = (place - local_ids) * block_faces
+    links = face_map + jnp.sum(
+        jnp.where(owner[None] == local_ids[:, None, None], shifts[:, None, None], 0), axis=0
+    )
 
     high, low = combined_matrix(members, rows, node_count)
     low_start = 2 * rows if not np.any(low[:, : 2 * rows].astype(np.float32)) else 0
     early = min(-(-(devices // 2) // 2), blocks // 2)
-    send_rows = round_up(3 * members, 8)
+    block_rows = round_up(3 * members * (node_count // 2), 8)
     return pl.pallas_call(
         lambda *refs: section_kernel(face_nodes, node_count, members, low_start, early, *refs),
         out_shape=(
             jax.ShapeDtypeStruct(water_depth.shape, f32),
             jax.ShapeDtypeStruct(momentum.shape, f32),
         ),
-        in_specs=[SMEM] * 8 + [VMEM] * 8,
+        in_specs=[SMEM] * 9 + [VMEM] * 8,
         out_specs=(VMEM, VMEM),
         scratch_shapes=[
             pltpu.VMEM((blocks // 2, 3, rows, lanes), f32),
@@ -533,10 +553,10 @@
             pltpu.VMEM((blocks, block_faces), f32),
             pltpu.VMEM((blocks, block_faces), f32),
             pltpu.VMEM((blocks, block_faces), f32),
-            pltpu.VMEM((high.shape[1], 3 * lanes), f32),
-            pltpu.VMEM((blocks, send_rows, node_cells), f32),
-            pltpu.VMEM((devices, send_rows, node_cells), f32),
-            pltpu.VMEM((devices, send_rows, node_cells), f32),
+            pltpu.VMEM((early, high.shape[1], 3 * lanes), f32),
+            pltpu.VMEM((blocks, block_rows, lanes), f32),
+            pltpu.VMEM((devices, block_rows, lanes), f32),
+            pltpu.VMEM((devices, block_rows, lanes), f32),
             pltpu.SemaphoreType.DMA((4,)),
             pltpu.SemaphoreType.DMA((devices,)),
             pltpu.SemaphoreType.DMA((devices,)),
@@ -545,7 +565,7 @@
             vmem_limit_bytes=48 * 2**20, collective_id=0, has_side_effects=True
         ),
     )(
-        order, to_place(face_map), to_place(rim_faces.reshape(-1)), wet_blocks, breach, chosen,
+        order, place, links, rim_faces, wet_blocks, breach.T, chosen,
         slot_place, source, water_depth, momentum, metric, face_scale, face_angle, face_map,
         jnp.asarray(high), jnp.asarray(low[:, low_start:]),
     )

time: 71.8 us -> 53.5 us (0.75)
  between operations: 15.8 us -> 0.82 us
  local copies, waits for them, and re-layouts: 7.67 us -> 5.49 us
  Pallas kernels: 44 us -> 43 us
    slice x2 -> x0, local copies, waits for them, and re-layouts: 1.42 us -> none  [to_place(): place[index] - index]
    pallas_call x1, Pallas kernels: 44 us -> 43 us  [body(): pl.pallas_call(lambda *refs: section_kernel(face_nodes, node_count, membe...]
    select_n x0 -> x1, other arithmetic: none -> 0.77 us  [body(): owner = face_map // block_faces]
    unnamed x19 -> x22, local copies, waits for them, and re-layouts: 3.58 us -> 2.82 us
    add x2 -> x1, other arithmetic: 1.51 us -> 0.75 us  [body(): face_map + jnp.sum(jnp.where(owner[None] == local_ids[:, None, None], shi...]
where the time goes in v2:
time: 53.5 us; the launch traced here: 53.2 us
  Pallas kernels  43 us (80%)
  local copies, waits for them, and re-layouts  5.49 us (10%)
  other arithmetic  3.87 us (7%)
  between operations  0.82 us (2%)
    pallas_call x1, Pallas kernels, body(): pl.pallas_call(lambda *refs: section_kernel(face_nodes, node_count, membe...  43 us
    unnamed x22, local copies, waits for them, and re-layouts  2.82 us
    pallas_call x2, local copies, waits for them, and re-layouts, body(): pl.pallas_call(lambda *refs: section_kernel(face_nodes, node_count, membe...  2.67 us

profile of v2, /device:TPU:13, one launch (start us, length us, event | category | flops | bytes accessed | tf_op | source)
XLA Modules:
  0.0 53.2 jit_solution(16957132134830005996)
XLA Ops:
  0.6 0.0 copy-start.9
  0.7 1.0 %select_reduce_fusion.1 = s32[24]{0:T(128)S(1)} fusion(s32[384]{0:T(512)} %param.21, s32[24]{0:T(128)S(1)} %iota_add_fusion), kind=kLoop, calls=%fused_computation.3 | loop fusion | flops 27624 | bytes 1728 | tf_op jit(solution)/shard_map/reduce_sum | solution.py:520
  1.6 0.8 %fusion.1 = (s32[24]{0:T(128)S(1)}, s32[24]{0:T(128)S(1)}) fusion(s32[]{:T(128)S(6)} %axis_index.12, s32[384]{0:T(512)} %param.21, s32[]{:T(128)S(6)} %select_n.39), kind=kLoop, calls=%fused_computation.18 | loop fusion | flops 264 | bytes 296 | tf_op jit(solution)/shard_map/add | solution.py:512
  2.4 0.2 convert_reduce_fusion.refs_1_
  2.6 0.1 select_reduce_fusion.4
  2.7 0.2 select_reduce_fusion.2
  2.9 0.8 %add_select_fusion = s32[24,192]{1,0:T(8,128)S(1)} fusion(s32[24,192]{1,0:T(8,128)} %refs_14_.1), kind=kLoop, calls=%fused_computation.2 | loop fusion | flops 36864 | bytes 36864 | tf_op jit(solution)/shard_map/jit(floor_divide)/jit(_where)/select_n | solution.py:527
  3.7 0.1 select_reduce_fusion
  3.8 0.7 %add.24.refs_2_ = s32[24,192]{1,0:T(8,128)S(1)} add(s32[24,192]{1,0:T(8,128)} %refs_14_.1, s32[24,192]{1,0:T(8,128)S(1)} %select_reduce_fusion) | non-fusion elementwise | flops 4608 | bytes 55296 | tf_op jit(solution)/shard_map/add | solution.py:529
  4.6 1.2 %copy.18.refs_9_ = f32[24,10,640]{2,1,0:T(8,128)S(1)} copy(f32[24,10,640]{2,0,1:T(8,128)} %param.12) | data formatting | bytes 1228800 | tf_op args[0]
  5.8 0.0 copy-done.9
  5.8 0.0 copy-start
  5.8 0.0 copy-start.1
  5.8 0.0 copy-start.2
  5.8 0.0 copy-start.3
  5.8 0.0 copy-start.4
  5.9 0.0 copy-start.5
  5.9 0.0 copy-start.6
  5.9 0.0 copy-start.7
  5.9 0.0 copy-start.8
  5.9 1.5 %copy.19.refs_10_ = f32[24,2,10,640]{3,2,1,0:T(8,128)} copy(f32[24,2,10,640]{3,1,2,0:T(2,128)S(1)} %copy-done.9) | data formatting | bytes 2457600 | tf_op args[1]
  7.4 0.0 copy-done
  7.4 0.0 copy-done.1
  7.4 0.0 copy-done.2
  7.4 0.0 copy-done.4
  7.5 0.0 copy-done.5
  7.5 0.0 copy-done.6
  7.5 0.0 copy-done.7
  7.5 0.0 copy-done.8
  7.5 43.0 %shard_map.131 = (f32[24,10,640]{2,1,0:T(8,128)S(1)}, f32[24,2,10,640]{3,2,1,0:T(8,128)S(1)}) custom-call(s32[24]{0:T(128)S(1)} %get-tuple-element.7.refs_0_, s32[24]{0:T(128)S(1)} %convert_reduce_fusion.refs_1_, s32[24,192]{1,0:T(8,128)S(1)} %add.24.refs_2_, s32[1,128]{1,0:T(1,128)S(1)} %copy-done.7, s32[24]{0:T(128)S(1)} %copy-done.8, ...), custom_call_target="tpu_custom_call" | custom-call | tf_op jit(solution)/shard_map/pallas_call | solution.py:537
  50.5 1.0 %copy.20 = f32[24,10,640]{2,0,1:T(8,128)} copy(f32[24,10,640]{2,1,0:T(8,128)S(1)} %get-tuple-element.4) | data formatting | bytes 1228800 | tf_op jit(solution)/shard_map/pallas_call | solution.py:537
  51.5 1.7 %copy.21 = f32[24,2,10,640]{3,1,2,0:T(2,128)} copy(f32[24,2,10,640]{3,2,1,0:T(8,128)S(1)} %get-tuple-element.5) | data formatting | bytes 2457600 | tf_op jit(solution)/shard_map/pallas_call | solution.py:537
  (5 shorter events, 0.0 us)
Async XLA Ops:
  0.6 5.2 %copy-start.9 = (f32[24,2,10,640]{3,1,2,0:T(2,128)S(1)}, f32[24,2,10,640]{3,1,2,0:T(2,128)}, u32[]{:S(2)}) copy-start(f32[24,2,10,640]{3,1,2,0:T(2,128)} %param.13) | copy-start | bytes 3686404
  5.8 1.6 %copy-start = (s32[24,192]{1,0:T(8,128)S(1)}, s32[24,192]{1,0:T(8,128)}, u32[]{:S(2)}) copy-start(s32[24,192]{1,0:T(8,128)} %refs_14_.1) | copy-start | bytes 55300
  5.8 1.6 %copy-start.1 = (bf16[112,352]{1,0:T(8,128)(2,1)S(1)}, bf16[112,352]{1,0:T(8,128)(2,1)}, u32[]{:S(2)}) copy-start(bf16[112,352]{1,0:T(8,128)(2,1)} %constant.39.clone.refs_16_) | copy-start | bytes 236548
  5.8 1.6 %copy-start.2 = (bf16[112,352]{1,0:T(8,128)(2,1)S(1)}, bf16[112,352]{1,0:T(8,128)(2,1)}, u32[]{:S(2)}) copy-start(bf16[112,352]{1,0:T(8,128)(2,1)} %constant.38.clone.refs_15_) | copy-start | bytes 236548
  5.8 1.6 %copy-start.3 = (f32[24,4,64]{2,1,0:T(4,128)S(1)}, f32[24,4,64]{2,1,0:T(4,128)}, u32[]{:S(2)}) copy-start(f32[24,4,64]{2,1,0:T(4,128)} %refs_11_.1) | copy-start | bytes 73732
  5.8 1.6 %copy-start.4 = (f32[24,192]{1,0:T(8,128)S(1)}, f32[24,192]{1,0:T(8,128)}, u32[]{:S(2)}) copy-start(f32[24,192]{1,0:T(8,128)} %refs_12_.1) | copy-start | bytes 55300
  5.9 1.6 %copy-start.5 = (f32[24,192]{1,0:T(8,128)S(1)}, f32[24,192]{1,0:T(8,128)}, u32[]{:S(2)}) copy-start(f32[24,192]{1,0:T(8,128)} %refs_13_.1) | copy-start | bytes 55300
  5.9 1.6 %copy-start.6 = (s32[24,10]{0,1:T(8,128)S(1)}, s32[24,10]{0,1:T(8,128)}, u32[]{:S(2)}) copy-start(s32[24,10]{0,1:T(8,128)} %param.20) | copy-start | bytes 2884
  5.9 1.6 %copy-start.7 = (s32[1,128]{1,0:T(1,128)S(1)}, s32[1,128]{1,0:T(1,128)}, u32[]{:S(2)}) copy-start(s32[1,128]{1,0:T(1,128)} %refs_3_.1) | copy-start | bytes 1540
  5.9 1.6 %copy-start.8 = (s32[24]{0:T(128)S(1)}, s32[24]{0:T(128)}, u32[]{:S(2)}) copy-start(s32[24]{0:T(128)} %refs_4_.1) | copy-start | bytes 292

commit v3 on v2

--- a/solution.py
+++ b/solution.py
@@ -132,77 +132,73 @@
         ]
 
 
-def lay_out(
-    face_nodes, node_count, order_ref, place_ref, depth_ref, flow_ref, rim_ref,
-    fields_ref, table_ref, edge_ref, stack_ref,
-):
-    blocks, members, node_cells = depth_ref.shape
+def lay_out(pair, sides, node_count, depth_ref, flow_ref, fields_ref):
+    members, node_cells = depth_ref.shape[1:]
     elements = node_cells // node_count
     lanes = 2 * elements
     full = members // 8 * 8
     rest = members - full
     used = node_count * members
     rows = fields_ref.shape[2]
+    for comp in range(3):
+        fields_ref[pair, comp, used:rows, :] = jnp.ones((rows - used, lanes), jnp.float32)
+        for half in range(node_count // 2):
+            for first, size in ((0, full), (full, rest)):
+                cells = (pl.ds(first, size), pl.ds(half * lanes, lanes))
+                if comp == 0:
+                    one = depth_ref[(sides[0], *cells)]
+                    two = depth_ref[(sides[1], *cells)]
+                else:
+                    one = flow_ref[(sides[0], comp - 1, *cells)]
+                    two = flow_ref[(sides[1], comp - 1, *cells)]
+                low = lanes_low(one.shape, elements)
+                base = node_count * first + 2 * half * size
+                fields_ref[pair, comp, base : base + size, :] = jnp.where(
+                    low, one, pltpu.roll(two, elements, 1)
+                )
+                fields_ref[pair, comp, base + size : base + 2 * size, :] = jnp.where(
+                    low, pltpu.roll(one, elements, 1), two
+                )
+
+
+def make_table(
+    face_nodes, node_count, depth_ref, flow_ref, rim_ref, fields_ref, table_ref, edge_ref, stack_ref
+):
+    blocks, members, node_cells = depth_ref.shape
+    elements = node_cells // node_count
     face_rows = face_points * members
     stack_ref[...] = jnp.zeros_like(stack_ref)
-
-    def one_pair(pair, carry):
-        sides = (order_ref[2 * pair], order_ref[2 * pair + 1])
-        for comp in range(3):
-            fields_ref[pair, comp, used:rows, :] = jnp.ones((rows - used, lanes), jnp.float32)
-            for half in range(node_count // 2):
-                for first, size in ((0, full), (full, rest)):
-                    cells = (pl.ds(first, size), pl.ds(half * lanes, lanes))
-                    if comp == 0:
-                        one = depth_ref[(sides[0], *cells)]
-                        two = depth_ref[(sides[1], *cells)]
-                    else:
-                        one = flow_ref[(sides[0], comp - 1, *cells)]
-                        two = flow_ref[(sides[1], comp - 1, *cells)]
-                    low = lanes_low(one.shape, elements)
-                    base = node_count * first + 2 * half * size
-                    fields_ref[pair, comp, base : base + size, :] = jnp.where(
-                        low, one, pltpu.roll(two, elements, 1)
-                    )
-                    fields_ref[pair, comp, base + size : base + 2 * size, :] = jnp.where(
-                        low, pltpu.roll(one, elements, 1), two
-                    )
+    for pair in range(blocks // 2):
+        lay_out(pair, (2 * pair, 2 * pair + 1), node_count, depth_ref, flow_ref, fields_ref)
         for face in range(faces):
             nodes = [int(node) for node in face_nodes[face][::-1]]
+            stacked = stack_ref.at[pair % 2, face]
             for comp in range(3):
                 stack_face(
-                    fields_ref, pair, comp, nodes, members, node_count,
-                    stack_ref.at[face], comp * face_rows,
-                )
-            turned = stack_ref[face].T
-            start = pl.multiple_of((2 * pair * faces + face) * elements, 8)
-            table_ref[pl.ds(start, elements), :] = turned[:elements]
-            start = pl.multiple_of(((2 * pair + 1) * faces + face) * elements, 8)
-            table_ref[pl.ds(start, elements), :] = turned[elements:]
-        return carry
-
-    lax.fori_loop(0, blocks // 2, one_pair, 0)
-    rim_count = rim_ref.shape[1]
-    block_faces = faces * elements
+                    fields_ref, pair, comp, nodes, members, node_count, stacked, comp * face_rows
+                )
+            turned = stacked[...].T
+            for side in range(2):
+                start = ((2 * pair + side) * faces + face) * elements
+                table_ref[start : start + elements, :] = (
+                    turned[side * elements : (side + 1) * elements]
+                )
 
     def one_group(group, carry):
         for step in range(16):
             face = group * 16 + step
-            number = rim_ref[0, face]
-            block = number // block_faces
-            number = number + (place_ref[block] - block) * block_faces
-            edge_ref[pl.ds(face, 1), :] = table_ref[pl.ds(number, 1), :]
+            edge_ref[pl.ds(face, 1), :] = table_ref[pl.ds(rim_ref[0, face], 1), :]
         return carry
 
-    lax.fori_loop(0, rim_count // 16, one_group, 0)
+    lax.fori_loop(0, rim_ref.shape[1] // 16, one_group, 0)
 
 
 def section_kernel(
     face_nodes, node_count, members, low_start, early,
-    order_ref, place_ref, map_ref, rim_ref, wet_ref, breach_ref, chosen_ref, slot_ref, source_ref,
+    order_ref, map_ref, rim_ref, wet_ref, breach_ref, chosen_ref, slot_ref, source_ref,
     depth_ref, flow_ref, metric_ref, scale_ref, angle_ref, links_ref, high_ref, low_ref,
     depth_out, flow_out,
-    fields_ref, pool_ref, edge_ref, before_ref, after_ref, picked_ref, inner_ref,
+    natural_ref, fields_ref, pool_ref, edge_ref, before_ref, after_ref, picked_ref, inner_ref,
     cos_ref, sin_ref, wall_ref, right_ref, moved_ref, send_ref, got_ref,
     rim_sems, send_sems, got_sems,
 ):
@@ -228,9 +224,9 @@
             device_id_type=mesh_type,
         )
 
-    lay_out(
-        face_nodes, node_count, order_ref, place_ref, depth_ref, flow_ref, rim_ref,
-        fields_ref, pool_ref, edge_ref, inner_ref,
+    make_table(
+        face_nodes, node_count, depth_ref, flow_ref, rim_ref,
+        natural_ref, pool_ref, edge_ref, inner_ref,
     )
     pl.semaphore_wait(barrier, devices - 1)
 
@@ -267,6 +263,7 @@
 
     def volume(pair, right_ref):
         sides = (order_ref[2 * pair], order_ref[2 * pair + 1])
+        lay_out(pair, sides, node_count, depth_ref, flow_ref, fields_ref)
         factors = jnp.concatenate([metric_ref[sides[0]], metric_ref[sides[1]]], axis=1)
         height = fields_ref[pair, 0]
         flow_x = fields_ref[pair, 1]
@@ -285,11 +282,8 @@
                 factors[1:2] * flux_f[comp] + factors[3:4] * flux_g[comp]
             )
 
-    def early_volume(pair, carry):
+    for pair in range(early):
         volume(pair, right_ref.at[pair])
-        return carry
-
-    lax.fori_loop(0, early, early_volume, 0)
 
     @pl.when(own > 0)
     def _():
@@ -301,7 +295,7 @@
         to_before.wait_recv()
         pool_ref[local_faces + rim : local_faces + 2 * rim, :] = after_ref[...]
 
-    def one_pair(pair, right_ref):
+    def one_pair(pair, right_ref, picked_ref, inner_ref):
         sides = (order_ref[2 * pair], order_ref[2 * pair + 1])
         for side in range(2):
             for face in range(block_faces):
@@ -413,16 +407,13 @@
                     moved_ref[2 * pair + 1, base : base + size, :] = two
 
 
-    def early_pair(pair, carry):
-        one_pair(pair, right_ref.at[pair])
-        return carry
-
     def late_pair(pair, carry):
         volume(pair, right_ref.at[0])
-        one_pair(pair, right_ref.at[0])
+        one_pair(pair, right_ref.at[0], picked_ref.at[0], inner_ref.at[0])
         return carry
 
-    lax.fori_loop(0, early, early_pair, 0)
+    for pair in range(early):
+        one_pair(pair, right_ref.at[pair], picked_ref.at[pair % 2], inner_ref.at[pair % 2])
 
     def one_send(device, carry):
         send_ref[device] = moved_ref[chosen_ref[device]]
@@ -430,8 +421,11 @@
 
     lax.fori_loop(0, devices, one_send, 0)
     sends = []
-    for step in sorted(range(1, devices), key=lambda step: abs(step - devices // 2)):
-        target = lax.rem(own + step, devices)
+    half_devices = devices // 2
+    own_half = own // half_devices
+    for step in [*range(half_devices, devices), *range(1, half_devices)]:
+        side = own_half if step < half_devices else 1 - own_half
+        target = side * half_devices + lax.rem(own + step, half_devices)
         sends.append(
             pltpu.make_async_remote_copy(
                 src_ref=send_ref.at[target], dst_ref=got_ref.at[own],
@@ -524,12 +518,6 @@
     slot_place = jnp.sum(jnp.where(origin[:, None] == local_ids[None, :], place[None, :], 0), axis=1)
     source = source // blocks
 
-    owner = face_map // block_faces
-    shifts = (place - local_ids) * block_faces
-    links = face_map + jnp.sum(
-        jnp.where(owner[None] == local_ids[:, None, None], shifts[:, None, None], 0), axis=0
-    )
-
     high, low = combined_matrix(members, rows, node_count)
     low_start = 2 * rows if not np.any(low[:, : 2 * rows].astype(np.float32)) else 0
     early = min(-(-(devices // 2) // 2), blocks // 2)
@@ -540,16 +528,17 @@
             jax.ShapeDtypeStruct(water_depth.shape, f32),
             jax.ShapeDtypeStruct(momentum.shape, f32),
         ),
-        in_specs=[SMEM] * 9 + [VMEM] * 8,
+        in_specs=[SMEM] * 8 + [VMEM] * 8,
         out_specs=(VMEM, VMEM),
         scratch_shapes=[
+            pltpu.VMEM((blocks // 2, 3, rows, lanes), f32),
             pltpu.VMEM((blocks // 2, 3, rows, lanes), f32),
             pltpu.VMEM((local_faces + rim_count, lanes), f32),
             pltpu.VMEM((rim_count, lanes), f32),
             pltpu.VMEM((rim, lanes), f32),
             pltpu.VMEM((rim, lanes), f32),
-            pltpu.VMEM((2 * block_faces, lanes), f32),
-            pltpu.VMEM((faces, lanes, lanes), f32),
+            pltpu.VMEM((2, 2 * block_faces, lanes), f32),
+            pltpu.VMEM((2, faces, lanes, lanes), f32),
             pltpu.VMEM((blocks, block_faces), f32),
             pltpu.VMEM((blocks, block_faces), f32),
             pltpu.VMEM((blocks, block_faces), f32),
@@ -565,7 +554,7 @@
             vmem_limit_bytes=48 * 2**20, collective_id=0, has_side_effects=True
         ),
     )(
-        order, place, links, rim_faces, wet_blocks, breach.T, chosen,
+        order, face_map, rim_faces, wet_blocks, breach.T, chosen,
         slot_place, source, water_depth, momentum, metric, face_scale, face_angle, face_map,
         jnp.asarray(high), jnp.asarray(low[:, low_start:]),
     )

time: 53.5 us -> 50.6 us (0.946)
  the two profiles are of different devices: /device:TPU:13 before, /device:TPU:1 now
where the time goes in v3:
time: 50.6 us; the launch traced here: 50.3 us
  Pallas kernels  42.5 us (84%)
  local copies, waits for them, and re-layouts  4.8 us (9%)
  other arithmetic  2.23 us (4%)
  between operations  0.78 us (2%)
    pallas_call x1, Pallas kernels, body(): pl.pallas_call(lambda *refs: section_kernel(face_nodes, node_count, membe...  42.5 us
    pallas_call x2, local copies, waits for them, and re-layouts, body(): pl.pallas_call(lambda *refs: section_kernel(face_nodes, node_count, membe...  2.67 us
    unnamed x22, local copies, waits for them, and re-layouts  2.13 us

profile of v3, /device:TPU:1, one launch (start us, length us, event | category | flops | bytes accessed | tf_op | source)
XLA Modules:
  0.0 50.3 jit_solution(5831608585369577731)
XLA Ops:
  0.6 0.0 copy-start.9
  0.7 1.0 %select_reduce_fusion = s32[24]{0:T(128)S(1)} fusion(s32[384]{0:T(512)} %param.21, s32[24]{0:T(128)S(1)} %iota_add_fusion), kind=kLoop, calls=%fused_computation | loop fusion | flops 27624 | bytes 1728 | tf_op jit(solution)/shard_map/reduce_sum | solution.py:514
  1.6 0.8 %fusion = (s32[24]{0:T(128)S(1)}, s32[24]{0:T(128)S(1)}) fusion(s32[]{:T(128)S(6)} %axis_index.12, s32[384]{0:T(512)} %param.21, s32[]{:T(128)S(6)} %select_n.30), kind=kLoop, calls=%fused_computation.12 | loop fusion | flops 264 | bytes 296 | tf_op jit(solution)/shard_map/add | solution.py:506
  2.4 0.2 convert_reduce_fusion
  2.6 0.1 select_reduce_fusion.3
  2.7 0.2 select_reduce_fusion.1
  2.9 1.2 %copy.18.refs_8_ = f32[24,10,640]{2,1,0:T(8,128)S(1)} copy(f32[24,10,640]{2,0,1:T(8,128)} %param.12) | data formatting | bytes 1228800 | tf_op args[0]
  4.1 0.0 copy-done.9
  4.1 0.0 copy-start
  4.2 0.0 copy-start.1
  4.2 0.0 copy-start.2
  4.2 0.0 copy-start.3
  4.2 0.0 copy-start.4
  4.2 0.0 copy-start.5
  4.2 0.0 copy-start.6
  4.2 0.0 copy-start.7
  4.2 0.0 copy-start.8
  4.3 0.2 copy.19.refs_9_
  4.5 0.4 copy-done
  4.9 0.2 copy-done.1
  5.1 0.0 copy-done.2
  5.1 0.0 copy-done.3
  5.1 0.0 copy-done.4
  5.1 0.0 copy-done.5
  5.1 0.0 copy-done.6
  5.1 0.0 copy-done.7
  5.1 0.0 copy-done.8
  5.1 42.5 %shard_map.131 = (f32[24,10,640]{2,1,0:T(8,128)S(1)}, f32[24,2,10,640]{3,2,1,0:T(8,128)S(1)}) custom-call(s32[24]{0:T(128)S(1)} %get-tuple-element.7.refs_0_, s32[24,192]{1,0:T(8,128)S(1)} %copy-done, s32[1,128]{1,0:T(1,128)S(1)} %copy-done.7, s32[24]{0:T(128)S(1)} %copy-done.8, s32[10,24]{1,0:T(8,128)S(1)} %bitcast.1, s32[16]{0:T(128)S(1)} %compare_select_fusion.refs_5_, ...), custom_call_target="tpu_custom_call" | custom-call | tf_op jit(solution)/shard_map/pallas_call | solution.py:525
  47.7 1.0 %copy.20 = f32[24,10,640]{2,0,1:T(8,128)} copy(f32[24,10,640]{2,1,0:T(8,128)S(1)} %get-tuple-element.4) | data formatting | bytes 1228800 | tf_op jit(solution)/shard_map/pallas_call | solution.py:525
  48.7 1.7 %copy.21 = f32[24,2,10,640]{3,1,2,0:T(2,128)} copy(f32[24,2,10,640]{3,2,1,0:T(8,128)S(1)} %get-tuple-element.5) | data formatting | bytes 2457600 | tf_op jit(solution)/shard_map/pallas_call | solution.py:525
  (3 shorter events, 0.0 us)
Async XLA Ops:
  0.6 3.5 %copy-start.9 = (f32[24,2,10,640]{3,1,2,0:T(2,128)S(1)}, f32[24,2,10,640]{3,1,2,0:T(2,128)}, u32[]{:S(2)}) copy-start(f32[24,2,10,640]{3,1,2,0:T(2,128)} %param.13) | copy-start | bytes 3686404
  4.1 0.7 %copy-start = (s32[24,192]{1,0:T(8,128)S(1)}, s32[24,192]{1,0:T(8,128)}, u32[]{:S(2)}) copy-start(s32[24,192]{1,0:T(8,128)} %refs_13_.1) | copy-start | bytes 55300
  4.2 0.9 %copy-start.1 = (bf16[112,352]{1,0:T(8,128)(2,1)S(1)}, bf16[112,352]{1,0:T(8,128)(2,1)}, u32[]{:S(2)}) copy-start(bf16[112,352]{1,0:T(8,128)(2,1)} %constant.30.clone.refs_15_) | copy-start | bytes 236548
  4.2 0.9 %copy-start.2 = (bf16[112,352]{1,0:T(8,128)(2,1)S(1)}, bf16[112,352]{1,0:T(8,128)(2,1)}, u32[]{:S(2)}) copy-start(bf16[112,352]{1,0:T(8,128)(2,1)} %constant.29.clone.refs_14_) | copy-start | bytes 236548
  4.2 0.9 %copy-start.3 = (f32[24,4,64]{2,1,0:T(4,128)S(1)}, f32[24,4,64]{2,1,0:T(4,128)}, u32[]{:S(2)}) copy-start(f32[24,4,64]{2,1,0:T(4,128)} %refs_10_.1) | copy-start | bytes 73732
  4.2 0.9 %copy-start.4 = (f32[24,192]{1,0:T(8,128)S(1)}, f32[24,192]{1,0:T(8,128)}, u32[]{:S(2)}) copy-start(f32[24,192]{1,0:T(8,128)} %refs_11_.1) | copy-start | bytes 55300
  4.2 0.9 %copy-start.5 = (f32[24,192]{1,0:T(8,128)S(1)}, f32[24,192]{1,0:T(8,128)}, u32[]{:S(2)}) copy-start(f32[24,192]{1,0:T(8,128)} %refs_12_.1) | copy-start | bytes 55300
  4.2 0.9 %copy-start.6 = (s32[24,10]{0,1:T(8,128)S(1)}, s32[24,10]{0,1:T(8,128)}, u32[]{:S(2)}) copy-start(s32[24,10]{0,1:T(8,128)} %param.20) | copy-start | bytes 2884
  4.2 0.9 %copy-start.7 = (s32[1,128]{1,0:T(1,128)S(1)}, s32[1,128]{1,0:T(1,128)}, u32[]{:S(2)}) copy-start(s32[1,128]{1,0:T(1,128)} %refs_2_.1) | copy-start | bytes 1540
  4.2 0.9 %copy-start.8 = (s32[24]{0:T(128)S(1)}, s32[24]{0:T(128)}, u32[]{:S(2)}) copy-start(s32[24]{0:T(128)} %refs_3_.1) | copy-start | bytes 292

commit v4 on v3

--- a/solution.py
+++ b/solution.py
@@ -258,7 +258,10 @@
     )
     wall_ref[...] = jnp.where(links_ref[...] == own_number, 1.0, 0.0)
     right_ref[...] = jnp.zeros_like(right_ref)
-    moved_ref[...] = jnp.zeros_like(moved_ref)
+    filled = 3 * halves * members
+    spare = moved_ref.shape[1] - filled
+    if spare:
+        moved_ref[:, filled:, :] = jnp.zeros((blocks, spare, lanes), jnp.float32)
     got_ref[own] = jnp.zeros(got_ref.shape[1:], jnp.float32)
 
     def volume(pair, right_ref):
@@ -419,7 +422,7 @@
         send_ref[device] = moved_ref[chosen_ref[device]]
         return carry
 
-    lax.fori_loop(0, devices, one_send, 0)
+    lax.fori_loop(0, devices, one_send, 0, unroll=4)
     sends = []
     half_devices = devices // 2
     own_half = own // half_devices
@@ -461,7 +464,7 @@
                         flow_out[(slot, comp - 1, *cells)] = value
         return carry
 
-    lax.fori_loop(0, blocks, one_slot, 0)
+    lax.fori_loop(0, blocks, one_slot, 0, unroll=4)
     for copy in sends:
         copy.wait_send()
 
@@ -501,7 +504,11 @@
     f32 = jnp.float32
 
     local_ids = jnp.arange(blocks, dtype=jnp.int32)
-    targets = lax.dynamic_slice_in_dim(block_plan, own * blocks, blocks) // blocks
+    slot_ids = own * blocks + local_ids
+    every_slot = jnp.arange(block_plan.shape[0], dtype=jnp.int32)
+    targets = jnp.sum(
+        jnp.where(every_slot[None, :] == slot_ids[:, None], block_plan[None, :], 0), axis=1
+    ) // blocks
     stays = (targets == own).astype(jnp.int32)
     keys = stays * blocks + local_ids
     place = jnp.sum((keys[None, :] < keys[:, None]).astype(jnp.int32), axis=1)
@@ -509,8 +516,6 @@
     device_ids = jnp.arange(devices, dtype=jnp.int32)
     chosen = jnp.sum(jnp.where(targets[None, :] == device_ids[:, None], place[None, :], 0), axis=1)
     chosen = jnp.where(device_ids == own, 0, chosen)
-    slot_ids = own * blocks + local_ids
-    every_slot = jnp.arange(block_plan.shape[0], dtype=jnp.int32)
     source = jnp.sum(
         jnp.where(block_plan[None, :] == slot_ids[:, None], every_slot[None, :], 0), axis=1
     )

time: 50.6 us -> 49.6 us (0.980)
  other arithmetic: 2.23 us -> 1.46 us
    add x1 -> x0, other arithmetic: 0.77 us -> none  [body(): keys = stays * blocks + local_ids]
where the time goes in v4:
time: 49.6 us; the launch traced here: 49.4 us
  Pallas kernels  42.3 us (85%)
  local copies, waits for them, and re-layouts  4.8 us (10%)
  other arithmetic  1.46 us (3%)
  between operations  0.79 us (2%)
    pallas_call x1, Pallas kernels, body(): pl.pallas_call(lambda *refs: section_kernel(face_nodes, node_count, membe...  42.3 us
    pallas_call x2, local copies, waits for them, and re-layouts, body(): pl.pallas_call(lambda *refs: section_kernel(face_nodes, node_count, membe...  2.67 us
    unnamed x22, local copies, waits for them, and re-layouts  2.13 us

profile of v4, /device:TPU:1, one launch (start us, length us, event | category | flops | bytes accessed | tf_op | source)
XLA Modules:
  0.0 49.4 jit_solution(9450361560286188666)
XLA Ops:
  0.6 0.0 copy-start.9
  0.7 1.0 %select_reduce_fusion = (s32[24]{0:T(128)S(1)}, s32[24]{0:T(128)S(1)}) fusion(s32[384]{0:T(512)} %param.21, s32[24]{0:T(128)S(1)} %iota_add_fusion), kind=kLoop, calls=%fused_computation | loop fusion | flops 55248 | bytes 1824 | tf_op jit(solution)/shard_map/reduce_sum | solution.py:519
  1.6 0.2 convert_reduce_fusion
  1.8 0.1 select_reduce_fusion.4
  1.9 0.2 select_reduce_fusion.2
  2.1 1.2 %copy.18.refs_8_ = f32[24,10,640]{2,1,0:T(8,128)S(1)} copy(f32[24,10,640]{2,0,1:T(8,128)} %param.12) | data formatting | bytes 1228800 | tf_op args[0]
  3.4 0.0 copy-done.9
  3.4 0.0 copy-start
  3.4 0.0 copy-start.1
  3.4 0.0 copy-start.2
  3.4 0.0 copy-start.3
  3.4 0.0 copy-start.4
  3.4 0.0 copy-start.5
  3.5 0.0 copy-start.6
  3.5 0.0 copy-start.7
  3.5 0.0 copy-start.8
  3.5 0.2 copy.19.refs_9_
  3.7 0.4 copy-done
  4.1 0.2 copy-done.1
  4.3 0.0 copy-done.2
  4.3 0.0 copy-done.3
  4.3 0.0 copy-done.4
  4.3 0.0 copy-done.5
  4.3 0.0 copy-done.6
  4.3 0.0 copy-done.7
  4.4 0.0 copy-done.8
  4.4 42.3 %shard_map.131 = (f32[24,10,640]{2,1,0:T(8,128)S(1)}, f32[24,2,10,640]{3,2,1,0:T(8,128)S(1)}) custom-call(s32[24]{0:T(128)S(1)} %get-tuple-element.9.refs_0_, s32[24,192]{1,0:T(8,128)S(1)} %copy-done, s32[1,128]{1,0:T(1,128)S(1)} %copy-done.7, s32[24]{0:T(128)S(1)} %copy-done.8, s32[10,24]{1,0:T(8,128)S(1)} %bitcast.1, s32[16]{0:T(128)S(1)} %compare_select_fusion.refs_5_, ...), custom_call_target="tpu_custom_call" | custom-call | tf_op jit(solution)/shard_map/pallas_call | solution.py:530
  46.7 1.0 %copy.20 = f32[24,10,640]{2,0,1:T(8,128)} copy(f32[24,10,640]{2,1,0:T(8,128)S(1)} %get-tuple-element.4) | data formatting | bytes 1228800 | tf_op jit(solution)/shard_map/pallas_call | solution.py:530
  47.7 1.7 %copy.21 = f32[24,2,10,640]{3,1,2,0:T(2,128)} copy(f32[24,2,10,640]{3,2,1,0:T(8,128)S(1)} %get-tuple-element.5) | data formatting | bytes 2457600 | tf_op jit(solution)/shard_map/pallas_call | solution.py:530
  (3 shorter events, 0.0 us)
Async XLA Ops:
  0.6 2.7 %copy-start.9 = (f32[24,2,10,640]{3,1,2,0:T(2,128)S(1)}, f32[24,2,10,640]{3,1,2,0:T(2,128)}, u32[]{:S(2)}) copy-start(f32[24,2,10,640]{3,1,2,0:T(2,128)} %param.13) | copy-start | bytes 3686404
  3.4 0.7 %copy-start = (s32[24,192]{1,0:T(8,128)S(1)}, s32[24,192]{1,0:T(8,128)}, u32[]{:S(2)}) copy-start(s32[24,192]{1,0:T(8,128)} %refs_13_.1) | copy-start | bytes 55300
  3.4 0.9 %copy-start.1 = (bf16[112,352]{1,0:T(8,128)(2,1)S(1)}, bf16[112,352]{1,0:T(8,128)(2,1)}, u32[]{:S(2)}) copy-start(bf16[112,352]{1,0:T(8,128)(2,1)} %constant.28.clone.refs_15_) | copy-start | bytes 236548
  3.4 0.9 %copy-start.2 = (bf16[112,352]{1,0:T(8,128)(2,1)S(1)}, bf16[112,352]{1,0:T(8,128)(2,1)}, u32[]{:S(2)}) copy-start(bf16[112,352]{1,0:T(8,128)(2,1)} %constant.27.clone.refs_14_) | copy-start | bytes 236548
  3.4 0.9 %copy-start.3 = (f32[24,4,64]{2,1,0:T(4,128)S(1)}, f32[24,4,64]{2,1,0:T(4,128)}, u32[]{:S(2)}) copy-start(f32[24,4,64]{2,1,0:T(4,128)} %refs_10_.1) | copy-start | bytes 73732
  3.4 0.9 %copy-start.4 = (f32[24,192]{1,0:T(8,128)S(1)}, f32[24,192]{1,0:T(8,128)}, u32[]{:S(2)}) copy-start(f32[24,192]{1,0:T(8,128)} %refs_11_.1) | copy-start | bytes 55300
  3.4 0.9 %copy-start.5 = (f32[24,192]{1,0:T(8,128)S(1)}, f32[24,192]{1,0:T(8,128)}, u32[]{:S(2)}) copy-start(f32[24,192]{1,0:T(8,128)} %refs_12_.1) | copy-start | bytes 55300
  3.5 0.9 %copy-start.6 = (s32[24,10]{0,1:T(8,128)S(1)}, s32[24,10]{0,1:T(8,128)}, u32[]{:S(2)}) copy-start(s32[24,10]{0,1:T(8,128)} %param.20) | copy-start | bytes 2884
  3.5 0.9 %copy-start.7 = (s32[1,128]{1,0:T(1,128)S(1)}, s32[1,128]{1,0:T(1,128)}, u32[]{:S(2)}) copy-start(s32[1,128]{1,0:T(1,128)} %refs_2_.1) | copy-start | bytes 1540
  3.5 0.9 %copy-start.8 = (s32[24]{0:T(128)S(1)}, s32[24]{0:T(128)}, u32[]{:S(2)}) copy-start(s32[24]{0:T(128)} %refs_3_.1) | copy-start | bytes 292
